TPU v7x, 128 devices: a whole 4x4x4 slice. The times are simulated.
128 devices in a mesh: coil: 8 (over y, core), space: 16 (over z, x).
Axes of the slice: x: 4, y: 4, z: 4, core: 2. Of those that a mesh axis runs over, the one named last changes fastest.
Arguments:
- image: float32 [2, 8, 512, 512], P(None, None, 'space'), may hold values from -6 to 6
- residual: float32 [2, 8, 512, 512], P(None, None, 'space'), may hold values from -20 to 20
- direction: float32 [2, 8, 512, 512], P(None, None, 'space'), may hold values from -20 to 20
- sensitivity: bfloat16 [2, 32, 8, 512, 512], P(None, 'coil', None, 'space'), may hold values from -1.2 to 1.2
- sampling: int32 [512, 512], P(None, 'space'), may hold values from 0 to 1
Outputs:
- image_next: float32 [2, 8, 512, 512], P(None, None, 'space', 'coil')
- residual_next: float32 [2, 8, 512, 512], P(None, None, 'space', 'coil')
- direction_next: float32 [2, 8, 512, 512], P(None, None, 'space', 'coil')
All inputs are finite; a program needn't handle non-finite values.
Results may differ from a plain program's by a relative error of at most 0.0019.
Values may be sent and summed in bfloat16 or wider, within the bound.
No kernel may reach another device: no remote copies, remote signals or barrier semaphores. Data moves between devices by JAX's collectives and lax.ppermute only.
A program may use at most 128 MiB of HBM per device.

v0:
```python
import math

import jax
import jax.numpy as jnp
from jax import lax
from jax.sharding import PartitionSpec as P

ridge_weight = 0.1


def tables(length):
    counter = jnp.arange(length, dtype=jnp.int32)
    product_mod = counter[:, None] * counter[None, :] % length
    phase_angle = product_mod.astype(jnp.float32) * (2.0 * math.pi / length)
    norm_scale = 1.0 / math.sqrt(length)
    return (
        (jnp.cos(phase_angle) * norm_scale).astype(jnp.bfloat16),
        (jnp.sin(phase_angle) * norm_scale).astype(jnp.bfloat16),
    )


def transform(pattern, real_part, imag_part, cos_t, sin_t, orient):
    real_cos = jnp.einsum(pattern, real_part, cos_t, preferred_element_type=jnp.float32)
    real_sin = jnp.einsum(pattern, real_part, sin_t, preferred_element_type=jnp.float32)
    imag_cos = jnp.einsum(pattern, imag_part, cos_t, preferred_element_type=jnp.float32)
    imag_sin = jnp.einsum(pattern, imag_part, sin_t, preferred_element_type=jnp.float32)
    return (real_cos + orient * imag_sin, imag_cos - orient * real_sin)


def on_device(image, residual, direction, sensitivity, sampling):
    cos_y, sin_y = tables(direction.shape[3])
    cos_z, sin_z = tables(sampling.shape[0])
    keep_mask = sampling.astype(jnp.float32)
    sens_re = sensitivity[0].astype(jnp.float32)
    sens_im = sensitivity[1].astype(jnp.float32)
    dir_re = direction[0][None]
    dir_im = direction[1][None]
    coil_re = (sens_re * dir_re - sens_im * dir_im).astype(jnp.bfloat16)
    coil_im = (sens_re * dir_im + sens_im * dir_re).astype(jnp.bfloat16)
    spec_re, spec_im = transform("cxzn,nk->cxzk", coil_re, coil_im, cos_y, sin_y, 1.0)
    stacked = jnp.stack((spec_re, spec_im)).astype(jnp.bfloat16)
    pencil = lax.all_to_all(stacked, "space", split_axis=4, concat_axis=3, tiled=True)
    kz_re, kz_im = transform("cxny,nk->cxky", pencil[0], pencil[1], cos_z, sin_z, 1.0)
    kept_re = (kz_re * keep_mask).astype(jnp.bfloat16)
    kept_im = (kz_im * keep_mask).astype(jnp.bfloat16)
    back_re, back_im = transform("cxky,kn->cxny", kept_re, kept_im, cos_z, sin_z, -1.0)
    back_field = jnp.stack((back_re, back_im)).astype(jnp.bfloat16)
    slabs = lax.all_to_all(back_field, "space", split_axis=3, concat_axis=4, tiled=True)
    field_re, field_im = transform("cxzk,kn->cxzn", slabs[0], slabs[1], cos_y, sin_y, -1.0)
    partial_re = jnp.sum(sens_re * field_re + sens_im * field_im, axis=0)
    partial_im = jnp.sum(sens_re * field_im - sens_im * field_re, axis=0)
    partial_value = jnp.stack((partial_re, partial_im))
    y_width = direction.shape[3] // lax.axis_size("coil")
    y_start = lax.axis_index("coil") * y_width

    def own_part(field):
        return lax.dynamic_slice_in_dim(field, y_start, y_width, 3)

    combined = own_part(lax.psum(partial_value, "coil"))
    dir_own = own_part(direction)
    res_own = own_part(residual)
    img_own = own_part(image)
    applied = combined + ridge_weight * dir_own
    old_sq = lax.psum(jnp.sum(res_own * res_own), ("coil", "space"))
    curvature = lax.psum(jnp.sum(dir_own * applied), ("coil", "space"))
    step_len = old_sq / curvature
    residual_next = res_own - step_len * applied
    new_sq = lax.psum(jnp.sum(residual_next * residual_next), ("coil", "space"))
    image_next = img_own + step_len * dir_own
    direction_next = residual_next + new_sq / old_sq * dir_own
    return (image_next, residual_next, direction_next)


def solution(mesh):
    placed = (
        P(None, None, "space", None),
        P(None, None, "space", None),
        P(None, None, "space", None),
        P(None, "coil", None, "space", None),
        P(None, "space"),
    )
    return jax.shard_map(
        on_device,
        mesh=mesh,
        in_specs=placed,
        out_specs=(
            P(None, None, "space", "coil"),
            P(None, None, "space", "coil"),
            P(None, None, "space", "coil"),
        ),
        check_vma=False,
    )
```

profile of v0, /device:TPU:1, one launch (start us, length us, event | category | flops | bytes accessed | tf_op | source)
XLA Modules:
  0.0 510.4 jit_solution(2896985026278411952)
XLA Ops:
  27.8 12.0 %copy.12 = bf16[2,4,8,32,512]{3,2,1,0,4:T(8,128)(2,1)} copy(bf16[2,4,8,32,512]{4,3,2,1,0:T(8,128)(2,1)S(1)} %pad_maximum_fusion) | data formatting | bytes 4194304 | tf_op jit(solution)/shard_map/stack | solution.py:41
  39.8 14.5 %reshape.23 = bf16[16,2,32768]{2,1,0:T(2,128)(2,1)} reshape(bf16[512,2,4,8,32]{4,3,2,1,0:T(8,128)(2,1)} %bitcast.104) | data formatting | bytes 4194304
  54.3 8.6 %all-to-all-start = ((bf16[16,2,32768]{2,1,0:T(2,128)(2,1)}), bf16[16,2,32768]{2,1,0:T(2,128)(2,1)S(1)}, u32[]{:S(2)}, u32[]{:S(2)}) async-start(bf16[16,2,32768]{2,1,0:T(2,128)(2,1)} %reshape.23), calls=%async_computation | async-start | bytes 4194304 | tf_op jit(solution)/shard_map/all_to_all | solution.py:42
  63.1 30.2 %all-to-all-done = bf16[16,2,32768]{2,1,0:T(2,128)(2,1)S(1)} async-done(((bf16[16,2,32768]{2,1,0:T(2,128)(2,1)}), bf16[16,2,32768]{2,1,0:T(2,128)(2,1)S(1)}, u32[]{:S(2)}, u32[]{:S(2)}) %all-to-all-start) | async-done | bytes 2097184 | tf_op jit(solution)/shard_map/all_to_all | solution.py:42
  93.3 8.8 %reshape.24 = bf16[512,2,4,8,32]{4,3,2,1,0:T(8,128)(2,1)} reshape(bf16[16,2,32768]{2,1,0:T(2,128)(2,1)S(1)} %all-to-all-done) | data formatting | bytes 4194304
  102.2 12.0 %copy.21 = bf16[2,4,8,32,16,32]{3,4,5,2,1,0:T(8,128)(2,1)} copy(bf16[2,4,8,32,16,32]{3,2,1,0,5,4:T(8,128)(2,1)} %bitcast.106) | data formatting | bytes 4194304 | tf_op jit(solution)/shard_map/all_to_all | solution.py:42
  114.2 6.6 %fusion.131 = (bf16[1,4,8,16,32,32]{4,3,5,2,1,0:T(8,128)(2,1)}, bf16[1,4,8,16,32,32]{4,3,5,2,1,0:T(8,128)(2,1)}) fusion(bf16[2,4,8,16,32,32]{4,3,5,2,1,0:T(8,128)(2,1)} %bitcast.108), kind=kLoop, calls=%fused_computation.146 | loop fusion | bytes 4194304 | tf_op jit(solution)/shard_map/slice | solution.py:43
  120.8 5.9 %squeeze.14 = bf16[4,8,512,32]{2,3,1,0:T(8,128)(2,1)S(1)} reshape(bf16[1,4,8,16,32,32]{4,3,5,2,1,0:T(8,128)(2,1)} %get-tuple-element.11) | data formatting | bytes 2097152 | tf_op jit(solution)/shard_map/squeeze | solution.py:43
  126.7 6.4 %fusion.40 = f32[512,4,8,32]{0,3,2,1:T(8,128)} fusion(bf16[4,8,512,32]{2,3,1,0:T(8,128)(2,1)S(1)} %squeeze.14), kind=kOutput, calls=%fused_computation.55 | convolution fusion | flops 541065216 | bytes 3145728 | tf_op jit(solution)/shard_map/cxny,nk->cxky/dot_general | solution.py:23
  133.1 5.9 %squeeze.15 = bf16[4,8,512,32]{2,3,1,0:T(8,128)(2,1)S(1)} reshape(bf16[1,4,8,16,32,32]{4,3,5,2,1,0:T(8,128)(2,1)} %get-tuple-element.12) | data formatting | bytes 2097152 | tf_op jit(solution)/shard_map/squeeze | solution.py:43
  139.0 6.1 %fusion.36 = f32[512,4,8,32]{0,3,2,1:T(8,128)S(1)} fusion(bf16[4,8,512,32]{2,3,1,0:T(8,128)(2,1)S(1)} %squeeze.15), kind=kOutput, calls=%fused_computation.53 | convolution fusion | flops 541065216 | bytes 3145728 | tf_op jit(solution)/shard_map/cxny,nk->cxky/dot_general | solution.py:25
  145.2 5.6 %fusion.10 = bf16[4,8,512,32]{2,3,1,0:T(8,128)(2,1)S(1)} fusion(f32[512,4,8,32]{0,3,2,1:T(8,128)S(1)} %copy-done.7, bf16[4,8,512,32]{2,3,1,0:T(8,128)(2,1)S(1)} %squeeze.15, f32[512,32]{0,1:T(8,128)S(1)} %convert_element_type.114), kind=kOutput, calls=%fused_computation.33 | convolution fusion | flops 542638080 | bytes 4259840 | tf_op jit(solution)/shard_map/cxny,nk->cxky/dot_general | solution.py:26
  150.7 5.7 %fusion.38 = f32[512,4,8,32]{0,3,2,1:T(8,128)S(1)} fusion(bf16[4,8,512,32]{2,3,1,0:T(8,128)(2,1)S(1)} %fusion.10), kind=kOutput, calls=%fused_computation.54 | convolution fusion | flops 541065216 | bytes 3145728 | tf_op jit(solution)/shard_map/cxky,kn->cxny/dot_general | solution.py:23
  156.5 5.6 %fusion.11 = bf16[4,8,512,32]{2,3,1,0:T(8,128)(2,1)S(1)} fusion(f32[512,4,8,32]{0,3,2,1:T(8,128)S(1)} %fusion.36, bf16[4,8,512,32]{2,3,1,0:T(8,128)(2,1)S(1)} %squeeze.14, f32[512,32]{0,1:T(8,128)S(1)} %convert_element_type.114), kind=kOutput, calls=%fused_computation.34 | convolution fusion | flops 542638080 | bytes 4259840 | tf_op jit(solution)/shard_map/cxny,nk->cxky/dot_general | solution.py:24
  162.0 5.7 %fusion.34 = f32[512,4,8,32]{0,3,2,1:T(8,128)S(1)} fusion(bf16[4,8,512,32]{2,3,1,0:T(8,128)(2,1)S(1)} %fusion.11), kind=kOutput, calls=%fused_computation.52 | convolution fusion | flops 541065216 | bytes 3145728 | tf_op jit(solution)/shard_map/cxky,kn->cxny/dot_general | solution.py:25
  167.8 5.6 %fusion.12 = bf16[1,4,8,512,32]{3,4,2,1,0:T(8,128)(2,1)S(1)} fusion(f32[512,4,8,32]{0,3,2,1:T(8,128)S(1)} %fusion.38, bf16[4,8,512,32]{2,3,1,0:T(8,128)(2,1)S(1)} %fusion.11), kind=kOutput, calls=%fused_computation.35 | convolution fusion | flops 542638080 | bytes 4194304 | tf_op jit(solution)/shard_map/cxky,kn->cxny/dot_general | solution.py:26
  173.3 5.8 %fusion.13 = bf16[1,4,8,512,32]{3,4,2,1,0:T(8,128)(2,1)S(1)} fusion(f32[512,4,8,32]{0,3,2,1:T(8,128)S(1)} %fusion.34, bf16[4,8,512,32]{2,3,1,0:T(8,128)(2,1)S(1)} %fusion.10), kind=kOutput, calls=%fused_computation.36 | convolution fusion | flops 542638080 | bytes 4194304 | tf_op jit(solution)/shard_map/cxky,kn->cxny/dot_general | solution.py:24
  179.3 12.0 %copy.14 = bf16[2,4,8,512,32]{4,2,1,0,3:T(8,128)(2,1)} copy(bf16[2,4,8,512,32]{3,4,2,1,0:T(8,128)(2,1)S(1)} %pad_maximum_fusion.1) | data formatting | bytes 4194304 | tf_op jit(solution)/shard_map/stack | solution.py:47
  191.3 13.4 %reshape.25 = bf16[16,2,32768]{2,1,0:T(2,128)(2,1)S(1)} reshape(bf16[512,2,4,8,32]{4,3,2,1,0:T(8,128)(2,1)} %bitcast.105) | data formatting | bytes 4194304
  204.7 31.3 %all_to_all.30 = bf16[16,2,32768]{2,1,0:T(2,128)(2,1)} all-to-all(bf16[16,2,32768]{2,1,0:T(2,128)(2,1)S(1)} %reshape.25), channel_id=1, replica_groups=mesh['coil'=8,'space'=16] {'space'}, dimensions={0} | all-to-all | bytes 4194304 | tf_op jit(solution)/shard_map/all_to_all | solution.py:48
  236.0 12.9 %reshape.26 = bf16[512,2,4,8,32]{4,3,2,1,0:T(8,128)(2,1)} reshape(bf16[16,2,32768]{2,1,0:T(2,128)(2,1)} %all_to_all.30) | data formatting | bytes 4194304
  248.8 12.0 %copy.20 = bf16[2,4,8,16,32,32]{5,3,4,2,1,0:T(8,128)(2,1)} copy(bf16[2,4,8,16,32,32]{5,2,1,0,4,3:T(8,128)(2,1)} %bitcast.107) | data formatting | bytes 4194304 | tf_op jit(solution)/shard_map/all_to_all | solution.py:48
  260.8 6.6 %fusion.130 = (bf16[1,4,8,32,16,32]{5,4,3,2,1,0:T(8,128)(2,1)}, bf16[1,4,8,32,16,32]{5,4,3,2,1,0:T(8,128)(2,1)}) fusion(bf16[2,4,8,32,16,32]{5,4,3,2,1,0:T(8,128)(2,1)} %bitcast.109), kind=kLoop, calls=%fused_computation.145 | loop fusion | bytes 4194304 | tf_op jit(solution)/shard_map/slice | solution.py:49
  267.4 5.9 %squeeze.17 = bf16[4,8,32,512]{3,2,1,0:T(8,128)(2,1)S(1)} reshape(bf16[1,4,8,32,16,32]{5,4,3,2,1,0:T(8,128)(2,1)} %get-tuple-element.9) | data formatting | bytes 2097152 | tf_op jit(solution)/shard_map/squeeze | solution.py:49
  273.4 6.4 %fusion.30 = f32[4,8,32,512]{3,2,1,0:T(8,128)} fusion(bf16[4,8,32,512]{3,2,1,0:T(8,128)(2,1)S(1)} %squeeze.17), kind=kOutput, calls=%fused_computation.50 | convolution fusion | flops 541065216 | bytes 3145728 | tf_op jit(solution)/shard_map/cxzk,kn->cxzn/dot_general | solution.py:25
  279.7 5.9 %squeeze.16 = bf16[4,8,32,512]{3,2,1,0:T(8,128)(2,1)S(1)} reshape(bf16[1,4,8,32,16,32]{5,4,3,2,1,0:T(8,128)(2,1)} %get-tuple-element.10) | data formatting | bytes 2097152 | tf_op jit(solution)/shard_map/squeeze | solution.py:49
  285.7 5.8 %fusion.32 = f32[4,8,32,512]{3,2,1,0:T(8,128)S(1)} fusion(bf16[4,8,32,512]{3,2,1,0:T(8,128)(2,1)S(1)} %squeeze.16), kind=kOutput, calls=%fused_computation.51 | convolution fusion | flops 541065216 | bytes 3145728 | tf_op jit(solution)/shard_map/cxzk,kn->cxzn/dot_general | solution.py:23
  291.5 6.5 %multiply_subtract_fusion = f32[4,8,32,512]{3,2,1,0:T(8,128)S(1)} fusion(f32[4,8,32,512]{3,2,1,0:T(8,128)S(1)} %copy-done.6, bf16[4,8,32,512]{3,2,1,0:T(8,128)(2,1)S(1)} %squeeze.16), kind=kOutput, calls=%fused_computation.20 | convolution fusion | flops 542113792 | bytes 5242880 | tf_op jit(solution)/shard_map/cxzk,kn->cxzn/dot_general | solution.py:24
  298.0 6.0 %fusion.5 = (f32[8,32,512]{2,1,0:T(8,128)S(1)}, f32[8,32,512]{2,1,0:T(8,128)S(1)}) fusion(f32[4,8,32,512]{3,2,1,0:T(8,128)S(1)} %multiply_subtract_fusion, bf16[2,4,8,32,512]{4,3,2,1,0:T(8,128)(2,1)S(1)} %copy-done.5, f32[4,8,32,512]{3,2,1,0:T(8,128)S(1)} %fusion.32, bf16[4,8,32,512]{3,2,1,0:T(8,128)(2,1)S(1)} %squeeze.17), kind=kOutput, calls=%fused_computation.15 | convolution fusion | flops 547094528 | bytes 8388608 | tf_op jit(solution)/shard_map/cxzk,kn->cxzn/dot_general | solution.py:26
  306.3 58.7 %all-reduce.3.cloned.1.call-done = f32[2,8,32,512]{3,2,1,0:T(8,128)} async-done(((f32[2,8,32,512]{3,2,1,0:T(8,128)}), f32[2,8,32,512]{3,2,1,0:T(8,128)}) %all-reduce.3.cloned.1.call-update) | async-done | bytes 1048592 | tf_op jit(solution)/shard_map/psum | solution.py:59
  366.8 67.3 %all-reduce = (f32[]{:T(128)}, f32[]{:T(128)}) all-reduce(f32[]{:T(128)} %multiply_reduce_fusion.2, f32[]{:T(128)} %multiply_reduce_fusion.1), channel_id=1, replica_groups=mesh['coil'=8,'space'=16] {'coil','space'}, use_global_device_ids=true, to_apply=%region_1.2 | all-reduce | flops 2 | bytes 16 | tf_op jit(solution)/shard_map/psum | solution.py:64
  437.3 62.6 %psum.31 = f32[]{:T(128)} all-reduce(f32[]{:T(128)} %get-tuple-element.7), channel_id=1, replica_groups=mesh['coil'=8,'space'=16] {'coil','space'}, use_global_device_ids=true, to_apply=%region_8.9 | all-reduce | flops 1 | bytes 8 | tf_op jit(solution)/shard_map/psum | solution.py:68
  (31 shorter events, 28.9 us)
Async XLA Ops:
  7.2 1.9 copy-start.4
  54.3 8.8 %copy-start.3 = (s32[512,32]{0,1:T(8,128)S(1)}, s32[512,32]{0,1:T(8,128)}, u32[]{:S(2)}) copy-start(s32[512,32]{0,1:T(8,128)} %param.9) | copy-start | bytes 196612
  54.3 39.1 %all-to-all-start = ((bf16[16,2,32768]{2,1,0:T(2,128)(2,1)}), bf16[16,2,32768]{2,1,0:T(2,128)(2,1)S(1)}, u32[]{:S(2)}, u32[]{:S(2)}) async-start(bf16[16,2,32768]{2,1,0:T(2,128)(2,1)} %reshape.23), calls=%async_computation | async-start | bytes 4194304 | tf_op jit(solution)/shard_map/all_to_all | solution.py:42
  62.8 302.2 %all-reduce.3.cloned.1.call-start = ((), (), s32[]{:S(2)}) async-start(), calls=%async_computation.2 | async-start | bytes 2097152 | tf_op jit(solution)/shard_map/psum | solution.py:59
  139.0 6.1 %copy-start.7 = (f32[512,4,8,32]{0,3,2,1:T(8,128)S(1)}, f32[512,4,8,32]{0,3,2,1:T(8,128)}, u32[]{:S(2)}) copy-start(f32[512,4,8,32]{0,3,2,1:T(8,128)} %fusion.40) | copy-start | bytes 6291460
  285.7 5.9 %copy-start.6 = (f32[4,8,32,512]{3,2,1,0:T(8,128)S(1)}, f32[4,8,32,512]{3,2,1,0:T(8,128)}, u32[]{:S(2)}) copy-start(f32[4,8,32,512]{3,2,1,0:T(8,128)} %fusion.30) | copy-start | bytes 6291460
  291.5 6.5 %copy-start.5 = (bf16[2,4,8,32,512]{4,3,2,1,0:T(8,128)(2,1)S(1)}, bf16[2,4,8,32,512]{4,3,2,1,0:T(8,128)(2,1)}, u32[]{:S(2)}) copy-start(bf16[2,4,8,32,512]{4,3,2,1,0:T(8,128)(2,1)} %param.8) | copy-start | bytes 6291460
  304.0 1.6 copy-start.2
  304.0 61.0 %copy-start = (f32[2,8,32,512]{3,2,1,0:T(8,128)S(1)}, f32[2,8,32,512]{3,2,1,0:T(8,128)}, u32[]{:S(2)}) copy-start(f32[2,8,32,512]{3,2,1,0:T(8,128)} %param.7) | copy-start | bytes 3145732
  437.3 65.9 %copy-start.1 = (f32[2,8,32,64]{3,2,1,0:T(8,128)}, f32[2,8,32,64]{3,2,1,0:T(8,128)S(1)}, u32[]{:S(2)}) copy-start(f32[2,8,32,64]{3,2,1,0:T(8,128)S(1)} %get-tuple-element.8) | copy-start | bytes 393220
Sparse Core Ops, SparseCore 0:
  305.3 59.6 all-reduce.2
where the time goes:
time: 521 us; the launch traced here: 510 us
  blocking collectives  161 us (31%)
  local copies, waits for them, and re-layouts  137 us (26%)
  matrix products  89.6 us (17%)
  waiting for transfers between devices  89 us (17%)
  between operations  17.3 us (3%)
  starting transfers between devices  8.78 us (2%)
  other arithmetic  7.8 us (1%)
    psum x1, blocking collectives, on_device(): old_sq = lax.psum(jnp.sum(res_own * res_own), ('coil', 'space'))  67.3 us
    psum x1, blocking collectives, on_device(): new_sq = lax.psum(jnp.sum(residual_next * residual_next), ('coil', 'space'))  62.6 us
    psum x1, waiting for transfers between devices, on_device(): combined = own_part(lax.psum(partial_value, 'coil'))  58.7 us
    unnamed x20, local copies, waits for them, and re-layouts  50.5 us
    all_to_all x1, blocking collectives, on_device(): lax.all_to_all(back_field, 'space', split_axis=3, concat_axis=4, tiled=True)  31.3 us
    all_to_all x1, waiting for transfers between devices, on_device(): lax.all_to_all(stacked, 'space', split_axis=4, concat_axis=3, tiled=True)  30.2 us
    dot_general x4, matrix products, transform(): jnp.einsum(pattern, imag_part, cos_t, preferred_element_type=jnp.float32)  22.7 us
    dot_general x4, matrix products, transform(): jnp.einsum(pattern, real_part, cos_t, preferred_element_type=jnp.float32)  22.4 us
  transfers between devices with their start and end apart: 2, of which 2 were waited for; matrix products, arithmetic and copies ran while one was open for 0% of the time, Pallas kernels for 0%

commit v1 on v0

v1 whole, which is shorter than its diff:
```python
import math

import jax
import jax.numpy as jnp
import ml_dtypes
import numpy as np
from jax import lax
from jax.experimental import pallas as pl
from jax.experimental.pallas import tpu as pltpu
from jax.sharding import PartitionSpec as P

ridge_weight = 0.1
vmem_limit = 8 * 1024 * 1024


def tables(length):
    counter = np.arange(length, dtype=np.int32)
    product_mod = counter[:, None] * counter[None, :] % length
    phase_angle = product_mod.astype(np.float32) * np.float32(2.0 * math.pi / length)
    norm_scale = np.float32(1.0 / math.sqrt(length))
    return np.cos(phase_angle) * norm_scale, np.sin(phase_angle) * norm_scale


def fold_tables(length):
    cos_t, sin_t = tables(length)
    half = length // 2
    even, odd = np.arange(0, half, 2), np.arange(1, half, 2)
    low = np.concatenate([even, odd])
    high = np.where(low == 0, half, length - low)
    sine = sin_t[:, low].copy()
    sine[:, 0] = cos_t[:, half]
    fold = np.concatenate([cos_t[:, low], sine], axis=1)
    order = np.concatenate([low, high])
    pick = np.eye(length, dtype=np.float32)[:, order]
    outs = [fold, fold.T, pick, pick.T]
    for group in (even, odd):
        at = np.concatenate([group, np.where(group == 0, half, length - group)])
        cos_g, sin_g = cos_t[:half, at], sin_t[:half, at]
        block = np.block([[cos_g, -sin_g], [sin_g, cos_g]])
        outs += [block, block.T]
    return [np.ascontiguousarray(out).astype(ml_dtypes.bfloat16) for out in outs]


def pack_kernel(core_ref, sens_ref, dir_ref, mask_ref, out_ref, dir_s, mask_s, sems):
    core_rows = pl.ds(pl.multiple_of(core_ref[0] * 16, 16), 16)
    small = [
        pltpu.make_async_copy(dir_ref.at[:, :, core_rows, :], dir_s, sems.at[8]),
        pltpu.make_async_copy(mask_ref.at[core_rows, :], mask_s, sems.at[9]),
    ]
    large = [
        pltpu.make_async_copy(
            sens_ref.at[part, half * 2 + pick],
            out_ref.at[:, half, pl.ds((part * 2 + pick) * 32, 32), :],
            sems.at[pick * 4 + part * 2 + half],
        )
        for pick in range(2)
        for part in range(2)
        for half in range(2)
    ]
    for copy in small + large:
        copy.start()
    for copy in small:
        copy.wait()
    kept = mask_s[...].astype(jnp.bfloat16)
    for x in range(8):
        for half in range(2):
            for part in range(2):
                out_ref[x, half, pl.ds(128 + part * 16, 16), :] = dir_s[part, x].astype(jnp.bfloat16)
            out_ref[x, half, pl.ds(160, 16), :] = kept
    for copy in large:
        copy.wait()


def pack(core, sensitivity, direction, mask_t):
    hbm = pl.BlockSpec(memory_space=pltpu.HBM)
    return pl.pallas_call(
        pack_kernel,
        in_specs=[pl.BlockSpec(memory_space=pltpu.SMEM), hbm, hbm, hbm],
        out_specs=pl.BlockSpec(memory_space=pltpu.VMEM),
        out_shape=jax.ShapeDtypeStruct((8, 2, 176, 512), jnp.bfloat16),
        scratch_shapes=[
            pltpu.VMEM((2, 8, 16, 512), jnp.float32),
            pltpu.VMEM((16, 512), jnp.int32),
            pltpu.SemaphoreType.DMA((10,)),
        ],
        compiler_params=pltpu.CompilerParams(vmem_limit_bytes=60 * 1024 * 1024),
        name="pack",
    )(core, sensitivity, direction, mask_t)


def operator_kernel(
    coil_ref, got_ref, mate_ref, fold_ref, fold_t_ref, pick_ref, pick_t_ref,
    z_even_ref, y_even_ref, z_odd_ref, y_odd_ref, dir_ref, res_ref, img_ref,
    keep_ref, send_ref, own_ref,
    image_s, spec_s, even_s, odd_s, rows_s, mask_s, own_s, sems,
):
    size = 512
    half = 256
    f32 = jnp.float32
    bf16 = jnp.bfloat16
    core = coil_ref[0] % 2
    own_lanes = pl.ds(pl.multiple_of(coil_ref[0] // 2 * 128, 128), 128)
    own_copies = [
        pltpu.make_async_copy(ref.at[:, :, :, own_lanes], own_s.at[index], sems.at[index])
        for index, ref in enumerate((dir_ref, res_ref, img_ref))
    ]
    for copy in own_copies:
        copy.start()

    def dot(left, right):
        return jnp.dot(left, right, preferred_element_type=f32)

    for kind in range(3):
        rows_s[kind, :, core] = got_ref[:, pl.ds(128 + kind * 16, 16), :]
        rows_s[kind, :, 1 - core] = mate_ref[:, pl.ds(kind * 16, 16), :]

    mask_t = dot(pick_t_ref[...], rows_s[2].reshape(size, size)).astype(bf16)
    mask_s[...] = dot(mask_t, pick_ref[...]).T

    def sens(coil, part, block, lanes):
        rows = got_ref[pl.ds(block * 8, 8), pl.ds((part * 2 + coil) * 32, 32), lanes]
        return rows.reshape(half, -1).astype(f32)

    first_lane = lax.broadcasted_iota(jnp.int32, (half, 128), 1) == 0
    for coil in range(2):
        for block in range(2):
            rows = pl.ds(block * half, half)
            for yb in range(2):
                cols = pl.ds(yb * half, half)
                dir_re, dir_im = (
                    rows_s[part, pl.ds(block * 8, 8), :, :, cols].reshape(half, half).astype(f32) for part in range(2)
                )
                sens_re, sens_im = (sens(coil, part, block, cols) for part in range(2))
                image_s[coil, 0, rows, cols] = (sens_re * dir_re - sens_im * dir_im).astype(bf16)
                image_s[coil, 1, rows, cols] = (sens_re * dir_im + sens_im * dir_re).astype(bf16)
            from_re = dot(image_s[coil, 0, rows, :], fold_ref[...])
            from_im = dot(image_s[coil, 1, rows, :], fold_ref[...])
            re_cos, re_sin = from_re[:, :half], from_re[:, half:]
            im_cos, im_sin = from_im[:, :half], from_im[:, half:]
            low = (re_cos + im_sin, im_cos - re_sin)
            high = (re_cos - im_sin, im_cos + re_sin)
            low_first = (re_cos, im_cos)
            high_first = (re_sin, im_sin)
            for part in range(2):
                for start, value, first in ((0, low[part], low_first[part]), (half, high[part], high_first[part])):
                    spec_s[coil, part, rows, pl.ds(start, 128)] = jnp.where(
                        first_lane, first[:, :128], value[:, :128]
                    ).astype(bf16)
                    spec_s[coil, part, rows, pl.ds(start + 128, 128)] = value[:, 128:].astype(bf16)

    first_row = lax.broadcasted_iota(jnp.int32, (128, half), 0) == 0
    for coil in range(2):
        for nb in range(2):
            cols = pl.ds(nb * half, half)
            from_re = dot(fold_t_ref[...], spec_s[coil, 0, :, cols])
            from_im = dot(fold_t_ref[...], spec_s[coil, 1, :, cols])

            def kept(group):
                rows = slice(group * 128, group * 128 + 128)
                rows_2 = slice(half + group * 128, half + group * 128 + 128)
                re_cos, re_sin = from_re[rows], from_re[rows_2]
                im_cos, im_sin = from_im[rows], from_im[rows_2]
                low = [re_cos + im_sin, im_cos - re_sin]
                high = [re_cos - im_sin, im_cos + re_sin]
                if group == 0:
                    low = [jnp.where(first_row, first, value) for first, value in zip((re_cos, im_cos), low)]
                    high = [jnp.where(first_row, first, value) for first, value in zip((re_sin, im_sin), high)]
                keep_low, keep_high = mask_s[rows, cols], mask_s[rows_2, cols]
                pieces = [low[0] * keep_low, high[0] * keep_high, low[1] * keep_low, high[1] * keep_high]
                return jnp.concatenate([piece.astype(bf16) for piece in pieces], axis=0)

            even = dot(z_even_ref[...], kept(0))
            odd = dot(z_odd_ref[...], kept(1))
            for part in range(2):
                rows = slice(part * half, part * half + half)
                back = ((even[rows] + odd[rows]).astype(bf16), (even[rows] - odd[rows]).astype(bf16))
                at = pl.ds(part * half + nb * 128, 128)
                for block in range(2):
                    even_s[coil, pl.ds(block * half, half), at] = back[block][:, :128]
                    odd_s[coil, pl.ds(block * half, half), at] = back[block][:, 128:]

    for copy in own_copies:
        copy.wait()
    lower = lax.broadcasted_iota(jnp.int32, (half, 128), 1) < 64

    def paired(re, im):
        even = jnp.where(lower, re, pltpu.roll(im, 64, 1))
        odd = jnp.where(lower, pltpu.roll(re, 64, 1), im)
        return even, odd

    for index in range(3):
        even, odd = paired(*(own_s[index, part].reshape(half, 128) for part in range(2)))
        own_ref[index] = jnp.where(core == 0, even, odd).reshape(8, 32, 128)

    for block in range(2):
        rows = pl.ds(block * half, half)
        sums = [[jnp.zeros((half, half), f32) for _ in range(2)] for _ in range(2)]
        for coil in range(2):
            even = dot(even_s[coil, rows, :], y_even_ref[...])
            odd = dot(odd_s[coil, rows, :], y_odd_ref[...])
            for yb in range(2):
                full = even + odd if yb == 0 else even - odd
                re, im = full[:, :half], full[:, half:]
                sens_re, sens_im = (sens(coil, part, block, pl.ds(yb * half, half)) for part in range(2))
                sums[yb][0] += sens_re * re + sens_im * im
                sums[yb][1] += sens_re * im - sens_im * re
        for yb in range(2):
            for lb in range(2):
                lanes = slice(lb * 128, lb * 128 + 128)
                even, odd = paired(sums[yb][0][:, lanes], sums[yb][1][:, lanes])
                slabs = pl.ds(block * 8, 8)
                keep_ref[slabs, yb * 2 + lb] = jnp.where(core == 0, even, odd).reshape(8, 32, 128)
                send_ref[slabs, yb * 2 + lb] = jnp.where(core == 0, odd, even).reshape(8, 32, 128)


def operator(coil, got, mate, fold_tabs, direction, residual, image):
    hbm = pl.BlockSpec(memory_space=pltpu.HBM)
    smem = pl.BlockSpec(memory_space=pltpu.SMEM)
    vmem = pl.BlockSpec(memory_space=pltpu.VMEM)
    return pl.pallas_call(
        operator_kernel,
        in_specs=[smem] + [vmem] * 10 + [hbm] * 3,
        out_specs=[vmem] * 3,
        out_shape=[
            jax.ShapeDtypeStruct((16, 4, 32, 128), jnp.float32),
            jax.ShapeDtypeStruct((16, 4, 32, 128), jnp.float32),
            jax.ShapeDtypeStruct((3, 8, 32, 128), jnp.float32),
        ],
        scratch_shapes=[
            pltpu.VMEM((2, 2, 512, 512), jnp.bfloat16),
            pltpu.VMEM((2, 2, 512, 512), jnp.bfloat16),
            pltpu.VMEM((2, 512, 512), jnp.bfloat16),
            pltpu.VMEM((2, 512, 512), jnp.bfloat16),
            pltpu.VMEM((3, 16, 2, 16, 512), jnp.bfloat16),
            pltpu.VMEM((512, 512), jnp.float32),
            pltpu.VMEM((3, 2, 8, 32, 128), jnp.float32),
            pltpu.SemaphoreType.DMA((3,)),
        ],
        compiler_params=pltpu.CompilerParams(vmem_limit_bytes=32 * 1024 * 1024),
        name="operator",
    )(coil, got, mate, *fold_tabs, direction, residual, image)


def sums_kernel(part_ref, own_ref, applied_ref, sums_ref):
    def body(x, carry):
        rr, da, ra, aa = carry
        total = jnp.zeros(applied_ref.shape[1:], jnp.float32)
        for coil in range(4):
            for pair in range(2):
                total += part_ref[x, pair, coil].astype(jnp.float32)
        direction = own_ref[0, x]
        residual = own_ref[1, x]
        applied = total + ridge_weight * direction
        applied_ref[x] = applied
        return (
            rr + residual * residual,
            da + direction * applied,
            ra + residual * applied,
            aa + applied * applied,
        )

    zero = jnp.zeros(applied_ref.shape[1:], jnp.float32)
    sums = lax.fori_loop(0, applied_ref.shape[0], body, (zero,) * 4)
    lane = lax.broadcasted_iota(jnp.int32, (1, 128), 1)
    row = jnp.zeros((1, 128), jnp.float32)
    for index, value in enumerate(sums):
        row = jnp.where(lane == index, jnp.sum(value), row)
    sums_ref[...] = jnp.broadcast_to(row, sums_ref.shape)


def final_kernel(all_ref, applied_ref, own_ref, img_out, res_out, dir_out):
    total = jnp.sum(all_ref[...], axis=0, keepdims=True)
    rr, da, ra, aa = (total[:, i : i + 1] for i in range(4))
    step = rr / da
    new = rr + step * (step * aa - 2.0 * ra)
    beta = new / rr
    step = step.reshape(1, 1, 1)
    beta = beta.reshape(1, 1, 1)
    direction = own_ref[0]
    img = own_ref[2] + step * direction
    res = own_ref[1] - step * applied_ref[...]
    nxt = res + beta * direction
    for out, value in ((img_out, img), (res_out, res), (dir_out, nxt)):
        out[0] = value[:, :, :64]
        out[1] = value[:, :, 64:]


def on_device(image, residual, direction, sensitivity, sampling):
    fold_tabs = [jnp.asarray(table) for table in fold_tables(512)]
    coil = lax.axis_index("coil").reshape(1)
    mates = [(at, at ^ 1) for at in range(8)]
    same_core = [[at * 16 + to for to in range(16) for at in range(side, 8, 2)] for side in range(2)]
    packed = pack(coil % 2, sensitivity, direction, sampling.T)
    got = lax.all_to_all(packed.reshape(16, 176, 512), "space", 0, 0, tiled=True)
    mate = lax.ppermute(got[:, 128:], "coil", mates)
    keep, send, own = operator(coil, got, mate, fold_tabs, direction, residual, image)
    pair_sum = (keep + lax.ppermute(send, "coil", mates)).astype(jnp.bfloat16)
    parts = lax.all_to_all(
        pair_sum.reshape(64, 32, 128), ("coil", "space"), 0, 0, axis_index_groups=same_core, tiled=True
    )
    whole = pl.BlockSpec(memory_space=pltpu.VMEM)
    params = pltpu.CompilerParams(vmem_limit_bytes=vmem_limit)
    applied, sums = pl.pallas_call(
        sums_kernel,
        in_specs=[whole] * 2,
        out_specs=[whole] * 2,
        out_shape=[
            jax.ShapeDtypeStruct((8, 32, 128), jnp.float32),
            jax.ShapeDtypeStruct((128, 128), jnp.float32),
        ],
        compiler_params=params,
        name="sums",
    )(parts.reshape(8, 2, 4, 32, 128), own)
    everyone = lax.all_to_all(sums, ("space", "coil"), split_axis=0, concat_axis=0, tiled=True)
    outs = pl.pallas_call(
        final_kernel,
        in_specs=[whole] * 3,
        out_specs=[whole] * 3,
        out_shape=[jax.ShapeDtypeStruct((2, 8, 32, 64), jnp.float32)] * 3,
        compiler_params=params,
        name="final",
    )(everyone, applied, own)
    return tuple(outs)


def solution(mesh):
    placed = (
        P(None, None, "space", None),
        P(None, None, "space", None),
        P(None, None, "space", None),
        P(None, "coil", None, "space", None),
        P(None, "space"),
    )
    return jax.shard_map(
        on_device,
        mesh=mesh,
        in_specs=placed,
        out_specs=(P(None, None, "space", "coil"),) * 3,
        check_vma=False,
    )
```

time: 521 us -> 98.3 us (0.19); the launches traced: 510 us -> 98.1 us
  local copies, waits for them, and re-layouts: 137 us -> 0.13 us
  matrix products: 89.6 us -> 0 us
  waiting for transfers between devices: 89 us -> 4.2 us
  blocking collectives: 161 us -> 77.9 us
  between operations: 17.3 us -> 0.82 us
  Pallas kernels: 0 us -> 12.5 us
  other arithmetic: 7.8 us -> 0.23 us
  starting transfers between devices: 8.78 us -> 2.34 us
    psum x2 -> x0, blocking collectives: 130 us -> none  [the longest x1 67.3 us: on_device(): old_sq = lax.psum(jnp.sum(res_own * res_own), ('coil', 'space'))]
    dot_general x16 -> x0, matrix products: 89.6 us -> none  [the longest x4 22.7 us: transform(): jnp.einsum(pattern, imag_part, cos_t, preferred_element_type=jnp.float32)]
    psum x1 -> x0, waiting for transfers between devices: 58.7 us -> none  [on_device(): combined = own_part(lax.psum(partial_value, 'coil'))]
    unnamed x20 -> x22, local copies, waits for them, and re-layouts: 50.5 us -> 0.07 us
    all_to_all x1 -> x3, blocking collectives: 31.3 us -> 77.9 us  [the longest x1 44.7 us: on_device(): lax.all_to_all(packed.reshape(16, 176, 512), 'space', 0, 0, tiled=True)]
    all_to_all x1 -> x0, waiting for transfers between devices: 30.2 us -> none  [on_device(): lax.all_to_all(stacked, 'space', split_axis=4, concat_axis=3, tiled=True)]
    all_to_all x2 -> x0, local copies, waits for them, and re-layouts: 24 us -> none  [the longest x1 12 us: on_device(): lax.all_to_all(stacked, 'space', split_axis=4, concat_axis=3, tiled=True)]
    another operation x2 -> x0, local copies, waits for them, and re-layouts: 23.9 us -> none  [the longest x1 12 us: on_device(): back_field = jnp.stack((back_re, back_im)).astype(jnp.bfloat16)]
where the time goes in v1:
time: 98.3 us; the launch traced here: 98.1 us
  blocking collectives  77.9 us (79%)
  Pallas kernels  12.5 us (13%)
  waiting for transfers between devices  4.2 us (4%)
  starting transfers between devices  2.34 us (2%)
    all_to_all x1, blocking collectives, on_device(): lax.all_to_all(packed.reshape(16, 176, 512), 'space', 0, 0, tiled=True)  44.7 us
    all_to_all x1, blocking collectives, on_device(): lax.all_to_all(pair_sum.reshape(64, 32, 128), ('coil', 'space'), 0, 0, ax...  18.4 us
    all_to_all x1, blocking collectives, on_device(): lax.all_to_all(sums, ('space', 'coil'), split_axis=0, concat_axis=0, tile...  14.8 us
    pallas_call x1, Pallas kernels, operator(): pl.pallas_call(operator_kernel, in_specs=[smem] + [vmem] * 10 + [hbm] * 3...  7.77 us
    pallas_call x1, Pallas kernels, pack(): pl.pallas_call(pack_kernel, in_specs=[pl.BlockSpec(memory_space=pltpu.SME...  3.36 us
    ppermute x1, waiting for transfers between devices, on_device(): pair_sum = (keep + lax.ppermute(send, 'coil', mates)).astype(jnp.bfloat16)  2.29 us
  transfers between devices with their start and end apart: 2, of which 2 were waited for; matrix products, arithmetic and copies ran while one was open for 0% of the time, Pallas kernels for 0%

profile of v1, /device:TPU:1, one launch (start us, length us, event | category | flops | bytes accessed | tf_op | source)
XLA Modules:
  0.0 98.1 jit_solution(10659393913845775368)
XLA Ops:
  0.6 3.4 %pack.1 = bf16[8,2,176,512]{3,2,1,0:T(8,128)(2,1)} custom-call(s32[1]{0:T(128)S(6)} %select_n.7.core_ref, bf16[2,4,8,32,512]{4,3,2,1,0:T(8,128)(2,1)} %sens_ref.1, f32[2,8,32,512]{3,2,1,0:T(8,128)} %dir_ref.3, s32[32,512]{1,0:T(8,128)} %bitcast.14), custom_call_target="tpu_custom_call" | custom-call | tf_op jit(solution)/shard_map/pack/pallas_call | solution.py:76
  4.0 0.0 copy-start
  4.0 0.0 copy-start.1
  4.0 0.0 copy-start.2
  4.0 0.0 copy-start.3
  4.1 0.0 copy-start.4
  4.1 0.0 copy-start.5
  4.1 0.0 copy-start.6
  4.1 0.0 copy-start.7
  4.1 0.0 copy-start.8
  4.1 0.0 copy-start.9
  4.1 0.0 copy-start.10
  4.1 44.7 %all_to_all.21.got_ref = bf16[16,176,512]{2,1,0:T(8,128)(2,1)S(1)} all-to-all(bf16[16,176,512]{2,1,0:T(8,128)(2,1)} %bitcast.12), channel_id=1, replica_groups=mesh['coil'=8,'space'=16] {'space'}, dimensions={0} | all-to-all | bytes 5767168 | tf_op jit(solution)/shard_map/all_to_all | solution.py:294
  48.8 0.1 slice.4
  48.9 1.9 %collective-permute-start = (bf16[16,48,512]{2,1,0:T(8,128)(2,1)S(1)}, bf16[16,48,512]{2,1,0:T(8,128)(2,1)S(1)}, u32[]{:S(2)}, u32[]{:S(2)}) collective-permute-start(bf16[16,48,512]{2,1,0:T(8,128)(2,1)S(1)} %slice.4), channel_id=1, source_target_pairs={{0,16},{16,0},{32,48},{48,32},{64,80},{80,64},{96,112},{112,96},{1... | collective-permute-start | bytes 2359304 | tf_op jit(solution)/shard_map/ppermute | solution.py:295
  50.7 1.9 %collective-permute-done.mate_ref = bf16[16,48,512]{2,1,0:T(8,128)(2,1)S(1)} collective-permute-done((bf16[16,48,512]{2,1,0:T(8,128)(2,1)S(1)}, bf16[16,48,512]{2,1,0:T(8,128)(2,1)S(1)}, u32[]{:S(2)}, u32[]{:S(2)}) %collective-permute-start) | collective-permute-done | bytes 786464 | tf_op jit(solution)/shard_map/ppermute | solution.py:295
  52.7 0.0 copy-done
  52.7 0.0 copy-done.1
  52.7 0.0 copy-done.2
  52.7 0.0 copy-done.3
  52.7 0.0 copy-done.4
  52.7 0.0 copy-done.5
  52.7 0.0 copy-done.6
  52.7 0.0 copy-done.7
  52.7 7.8 %operator.1 = (f32[16,4,32,128]{3,2,1,0:T(8,128)S(1)}, f32[16,4,32,128]{3,2,1,0:T(8,128)S(1)}, f32[3,8,32,128]{3,2,1,0:T(8,128)S(1)}) custom-call(s32[1]{0:T(128)} %bitcast.coil_ref, bf16[16,176,512]{2,1,0:T(8,128)(2,1)S(1)} %all_to_all.21.got_ref, bf16[16,48,512]{2,1,0:T(8,128)(2,1)S(1)} %collective-permute-done.mate_ref, bf16[512,512]{1,0:T(8,128)(2,1)S(1)} %copy-done.10, ...), custom_call_target="tpu_custom_call" | custom-call | tf_op jit(solution)/shard_map/operator/pallas_call | solution.py:220
  60.5 0.5 collective-permute-start.1
  61.0 2.3 %collective-permute-done.1 = f32[16,4,32,128]{3,2,1,0:T(8,128)S(1)} collective-permute-done((f32[16,4,32,128]{3,2,1,0:T(8,128)S(1)}, f32[16,4,32,128]{3,2,1,0:T(8,128)S(1)}, u32[]{:S(2)}, u32[]{:S(2)}) %collective-permute-start.1) | collective-permute-done | bytes 1048608 | tf_op jit(solution)/shard_map/ppermute | solution.py:297
  63.3 0.2 add_convert_fusion
  63.5 18.4 %all_to_all.22 = bf16[64,32,128]{2,1,0:T(8,128)(2,1)S(1)} all-to-all(bf16[64,32,128]{2,1,0:T(8,128)(2,1)S(1)} %bitcast.13), channel_id=1, replica_groups={{0,32,64,96,1,33,65,97,2,34,66,98,3,35,67,99,4,36,68,100,5,37,69,101,6,..., dimensions={0} | all-to-all | bytes 1048576 | tf_op jit(solution)/shard_map/all_to_all | solution.py:298
  81.9 0.3 sums.1
  82.2 14.8 %all_to_all.23 = f32[128,1,128]{2,1,0:T(1,128)S(1)} all-to-all(f32[128,1,128]{2,1,0:T(1,128)S(1)} %bitcast.11), channel_id=1, replica_groups=mesh['coil'=8,'space'=16] {'space','coil'}, dimensions={0} | all-to-all | bytes 131072 | tf_op jit(solution)/shard_map/all_to_all | solution.py:314
  97.0 1.1 %final.1 = (f32[2,8,32,64]{3,2,1,0:T(8,128)}, f32[2,8,32,64]{3,2,1,0:T(8,128)}, f32[2,8,32,64]{3,2,1,0:T(8,128)}) custom-call(f32[128,128]{1,0:T(8,128)S(1)} %bitcast.10, f32[8,32,128]{2,1,0:T(8,128)S(1)} %get-tuple-element.12.applied_ref, f32[3,8,32,128]{3,2,1,0:T(8,128)S(1)} %get-tuple-element.10.own_ref), custom_call_target="tpu_custom_call" | custom-call | tf_op jit(solution)/shard_map/final/pallas_call | solution.py:315
  (3 shorter events, 0.0 us)
Async XLA Ops:
  4.0 48.7 %copy-start = (f32[2,8,32,512]{3,2,1,0:T(8,128)S(1)}, f32[2,8,32,512]{3,2,1,0:T(8,128)}, u32[]{:S(2)}) copy-start(f32[2,8,32,512]{3,2,1,0:T(8,128)} %dir_ref.3) | copy-start | bytes 3145732
  4.0 48.6 %copy-start.1 = (f32[2,8,32,512]{3,2,1,0:T(8,128)S(1)}, f32[2,8,32,512]{3,2,1,0:T(8,128)}, u32[]{:S(2)}) copy-start(f32[2,8,32,512]{3,2,1,0:T(8,128)} %res_ref.1) | copy-start | bytes 3145732
  4.0 48.6 %copy-start.2 = (f32[2,8,32,512]{3,2,1,0:T(8,128)S(1)}, f32[2,8,32,512]{3,2,1,0:T(8,128)}, u32[]{:S(2)}) copy-start(f32[2,8,32,512]{3,2,1,0:T(8,128)} %img_ref.1) | copy-start | bytes 3145732
  4.0 48.6 %copy-start.3 = (bf16[512,512]{1,0:T(8,128)(2,1)S(1)}, bf16[512,512]{1,0:T(8,128)(2,1)}, u32[]{:S(2)}) copy-start(bf16[512,512]{1,0:T(8,128)(2,1)} %constant.48.clone.y_odd_ref) | copy-start | bytes 1572868
  4.1 48.6 %copy-start.4 = (bf16[512,512]{1,0:T(8,128)(2,1)S(1)}, bf16[512,512]{1,0:T(8,128)(2,1)}, u32[]{:S(2)}) copy-start(bf16[512,512]{1,0:T(8,128)(2,1)} %constant.47.clone.z_odd_ref) | copy-start | bytes 1572868
  4.1 48.6 %copy-start.5 = (bf16[512,512]{1,0:T(8,128)(2,1)S(1)}, bf16[512,512]{1,0:T(8,128)(2,1)}, u32[]{:S(2)}) copy-start(bf16[512,512]{1,0:T(8,128)(2,1)} %constant.46.clone.y_even_ref) | copy-start | bytes 1572868
  4.1 48.6 %copy-start.6 = (bf16[512,512]{1,0:T(8,128)(2,1)S(1)}, bf16[512,512]{1,0:T(8,128)(2,1)}, u32[]{:S(2)}) copy-start(bf16[512,512]{1,0:T(8,128)(2,1)} %constant.45.clone.z_even_ref) | copy-start | bytes 1572868
  4.1 48.6 %copy-start.7 = (bf16[512,512]{1,0:T(8,128)(2,1)S(1)}, bf16[512,512]{1,0:T(8,128)(2,1)}, u32[]{:S(2)}) copy-start(bf16[512,512]{1,0:T(8,128)(2,1)} %constant.44.clone.pick_t_ref) | copy-start | bytes 1572868
  4.1 48.6 %copy-start.8 = (bf16[512,512]{1,0:T(8,128)(2,1)S(1)}, bf16[512,512]{1,0:T(8,128)(2,1)}, u32[]{:S(2)}) copy-start(bf16[512,512]{1,0:T(8,128)(2,1)} %constant.43.clone.pick_ref) | copy-start | bytes 1572868
  4.1 48.6 %copy-start.9 = (bf16[512,512]{1,0:T(8,128)(2,1)S(1)}, bf16[512,512]{1,0:T(8,128)(2,1)}, u32[]{:S(2)}) copy-start(bf16[512,512]{1,0:T(8,128)(2,1)} %constant.42.clone.fold_t_ref) | copy-start | bytes 1572868
  4.1 48.6 %copy-start.10 = (bf16[512,512]{1,0:T(8,128)(2,1)S(1)}, bf16[512,512]{1,0:T(8,128)(2,1)}, u32[]{:S(2)}) copy-start(bf16[512,512]{1,0:T(8,128)(2,1)} %constant.41.clone.fold_ref) | copy-start | bytes 1572868
  48.9 3.8 %collective-permute-start = (bf16[16,48,512]{2,1,0:T(8,128)(2,1)S(1)}, bf16[16,48,512]{2,1,0:T(8,128)(2,1)S(1)}, u32[]{:S(2)}, u32[]{:S(2)}) collective-permute-start(bf16[16,48,512]{2,1,0:T(8,128)(2,1)S(1)} %slice.4), channel_id=1, source_target_pairs={{0,16},{16,0},{32,48},{48,32},{64,80},{80,64},{96,112},{112,96},{1... | collective-permute-start | bytes 2359304 | tf_op jit(solution)/shard_map/ppermute | solution.py:295
  60.5 2.8 %collective-permute-start.1 = (f32[16,4,32,128]{3,2,1,0:T(8,128)S(1)}, f32[16,4,32,128]{3,2,1,0:T(8,128)S(1)}, u32[]{:S(2)}, u32[]{:S(2)}) collective-permute-start(f32[16,4,32,128]{3,2,1,0:T(8,128)S(1)} %get-tuple-element.9), channel_id=1, source_target_pairs={{0,16},{16,0},{32,48},{48,32},{64,80},{80,64},{96,112},{112,96},{1... | collective-permute-start | bytes 3145736 | tf_op jit(solution)/shard_map/ppermute | solution.py:297

commit v2 on v1

--- a/solution.py
+++ b/solution.py
@@ -41,33 +41,45 @@
     return [np.ascontiguousarray(out).astype(ml_dtypes.bfloat16) for out in outs]
 
 
-def pack_kernel(core_ref, sens_ref, dir_ref, mask_ref, out_ref, dir_s, mask_s, sems):
+def pack_kernel(core_ref, sens_ref, dir_ref, mask_ref, out_ref, sens_s, dir_s, mask_s, small_s, in_sems, out_sems):
     core_rows = pl.ds(pl.multiple_of(core_ref[0] * 16, 16), 16)
     small = [
-        pltpu.make_async_copy(dir_ref.at[:, :, core_rows, :], dir_s, sems.at[8]),
-        pltpu.make_async_copy(mask_ref.at[core_rows, :], mask_s, sems.at[9]),
-    ]
-    large = [
+        pltpu.make_async_copy(dir_ref.at[part, :, core_rows, :], dir_s.at[part], in_sems.at[8 + part])
+        for part in range(2)
+    ]
+    small.append(pltpu.make_async_copy(mask_ref.at[core_rows, :], mask_s, in_sems.at[10]))
+    pairs = [(part, coil) for part in range(2) for coil in range(4)]
+    loads = [
+        pltpu.make_async_copy(sens_ref.at[part, coil], sens_s.at[part, coil], in_sems.at[part * 4 + coil])
+        for part, coil in pairs
+    ]
+    stores = [
         pltpu.make_async_copy(
-            sens_ref.at[part, half * 2 + pick],
-            out_ref.at[:, half, pl.ds((part * 2 + pick) * 32, 32), :],
-            sems.at[pick * 4 + part * 2 + half],
+            sens_s.at[part, coil],
+            out_ref.at[:, coil // 2, pl.ds((part * 2 + coil % 2) * 32, 32), :],
+            out_sems.at[part * 4 + coil],
         )
-        for pick in range(2)
-        for part in range(2)
+        for part, coil in pairs
+    ]
+    stores += [
+        pltpu.make_async_copy(small_s, out_ref.at[:, half, pl.ds(128, 48), :], out_sems.at[8 + half])
         for half in range(2)
     ]
-    for copy in small + large:
+    for copy in small + loads:
         copy.start()
     for copy in small:
         copy.wait()
     kept = mask_s[...].astype(jnp.bfloat16)
     for x in range(8):
-        for half in range(2):
-            for part in range(2):
-                out_ref[x, half, pl.ds(128 + part * 16, 16), :] = dir_s[part, x].astype(jnp.bfloat16)
-            out_ref[x, half, pl.ds(160, 16), :] = kept
-    for copy in large:
+        for part in range(2):
+            small_s[x, pl.ds(part * 16, 16), :] = dir_s[part, x].astype(jnp.bfloat16)
+        small_s[x, pl.ds(32, 16), :] = kept
+    for copy in stores[8:]:
+        copy.start()
+    for load, store in zip(loads, stores):
+        load.wait()
+        store.start()
+    for copy in stores:
         copy.wait()
 
 
@@ -76,11 +88,14 @@
     return pl.pallas_call(
         pack_kernel,
         in_specs=[pl.BlockSpec(memory_space=pltpu.SMEM), hbm, hbm, hbm],
-        out_specs=pl.BlockSpec(memory_space=pltpu.VMEM),
+        out_specs=hbm,
         out_shape=jax.ShapeDtypeStruct((8, 2, 176, 512), jnp.bfloat16),
         scratch_shapes=[
+            pltpu.VMEM((2, 4, 8, 32, 512), jnp.bfloat16),
             pltpu.VMEM((2, 8, 16, 512), jnp.float32),
             pltpu.VMEM((16, 512), jnp.int32),
+            pltpu.VMEM((8, 48, 512), jnp.bfloat16),
+            pltpu.SemaphoreType.DMA((11,)),
             pltpu.SemaphoreType.DMA((10,)),
         ],
         compiler_params=pltpu.CompilerParams(vmem_limit_bytes=60 * 1024 * 1024),
@@ -88,11 +103,66 @@
     )(core, sensitivity, direction, mask_t)
 
 
+def dot(left, right):
+    return jnp.dot(left, right, preferred_element_type=jnp.float32)
+
+
+def spectrum_rows(got_ref, dir_parts, core, fold_ref, image_s, store):
+    half = 256
+    first_lane = lax.broadcasted_iota(jnp.int32, (half, 128), 1) == 0
+    for coil in range(2):
+        for yb in range(2):
+            cols = pl.ds(yb * half, half)
+            dir_re, dir_im = (part[:, :, cols].reshape(half, half).astype(jnp.float32) for part in dir_parts)
+            sens_re, sens_im = (
+                got_ref[:, pl.ds(pl.multiple_of((part * 2 + coil) * 32 + core * 16, 16), 16), cols]
+                .reshape(half, half)
+                .astype(jnp.float32)
+                for part in range(2)
+            )
+            image_s[coil, 0, :, cols] = (sens_re * dir_re - sens_im * dir_im).astype(jnp.bfloat16)
+            image_s[coil, 1, :, cols] = (sens_re * dir_im + sens_im * dir_re).astype(jnp.bfloat16)
+        from_re = dot(image_s[coil, 0], fold_ref[...])
+        from_im = dot(image_s[coil, 1], fold_ref[...])
+        re_cos, re_sin = from_re[:, :half], from_re[:, half:]
+        im_cos, im_sin = from_im[:, :half], from_im[:, half:]
+        low = (re_cos + im_sin, im_cos - re_sin)
+        high = (re_cos - im_sin, im_cos + re_sin)
+        low_first = (re_cos, im_cos)
+        high_first = (re_sin, im_sin)
+        for part in range(2):
+            for start, value, first in ((0, low[part], low_first[part]), (half, high[part], high_first[part])):
+                edge = jnp.where(first_lane, first[:, :128], value[:, :128])
+                store(coil, part, start, edge.astype(jnp.bfloat16))
+                store(coil, part, start + 128, value[:, 128:].astype(jnp.bfloat16))
+
+
+def own_rows_kernel(coil_ref, got_ref, fold_ref, out_ref, image_s):
+    def store(coil, part, start, value):
+        out_ref[coil, part, :, :, pl.ds(start, 128)] = value.reshape(16, 16, 128)
+
+    dir_parts = [got_ref.at[:, pl.ds(128 + part * 16, 16), :] for part in range(2)]
+    spectrum_rows(got_ref, dir_parts, coil_ref[0] % 2, fold_ref, image_s, store)
+
+
+def own_rows(coil, got, fold):
+    vmem = pl.BlockSpec(memory_space=pltpu.VMEM)
+    return pl.pallas_call(
+        own_rows_kernel,
+        in_specs=[pl.BlockSpec(memory_space=pltpu.SMEM), vmem, vmem],
+        out_specs=vmem,
+        out_shape=jax.ShapeDtypeStruct((2, 2, 16, 16, 512), jnp.bfloat16),
+        scratch_shapes=[pltpu.VMEM((2, 2, 256, 512), jnp.bfloat16)],
+        compiler_params=pltpu.CompilerParams(vmem_limit_bytes=16 * 1024 * 1024),
+        name="own_rows",
+    )(coil, got, fold)
+
+
 def operator_kernel(
-    coil_ref, got_ref, mate_ref, fold_ref, fold_t_ref, pick_ref, pick_t_ref,
+    coil_ref, got_ref, mate_ref, ready_ref, fold_ref, fold_t_ref, pick_ref, pick_t_ref,
     z_even_ref, y_even_ref, z_odd_ref, y_odd_ref, dir_ref, res_ref, img_ref,
     keep_ref, send_ref, own_ref,
-    image_s, spec_s, even_s, odd_s, rows_s, mask_s, own_s, sems,
+    image_s, spec_s, even_s, odd_s, mask_t_s, mask_s, own_s, sems,
 ):
     size = 512
     half = 256
@@ -107,53 +177,30 @@
     for copy in own_copies:
         copy.start()
 
-    def dot(left, right):
-        return jnp.dot(left, right, preferred_element_type=f32)
-
-    for kind in range(3):
-        rows_s[kind, :, core] = got_ref[:, pl.ds(128 + kind * 16, 16), :]
-        rows_s[kind, :, 1 - core] = mate_ref[:, pl.ds(kind * 16, 16), :]
-
-    mask_t = dot(pick_t_ref[...], rows_s[2].reshape(size, size)).astype(bf16)
+    mask_t_s[:, core] = got_ref[:, pl.ds(160, 16), :]
+    mask_t_s[:, 1 - core] = mate_ref[:, pl.ds(32, 16), :]
+    mask_t = dot(pick_t_ref[...], mask_t_s[...].reshape(size, size)).astype(bf16)
     mask_s[...] = dot(mask_t, pick_ref[...]).T
+
+    def store(coil, part, start, value):
+        spec_s[coil, part, :, 1 - core, :, pl.ds(start, 128)] = value.reshape(16, 16, 128)
+
+    dir_parts = [mate_ref.at[:, pl.ds(part * 16, 16), :] for part in range(2)]
+    spectrum_rows(got_ref, dir_parts, 1 - core, fold_ref, image_s, store)
+    for coil in range(2):
+        for part in range(2):
+            spec_s[coil, part, :, core] = ready_ref[coil, part]
 
     def sens(coil, part, block, lanes):
         rows = got_ref[pl.ds(block * 8, 8), pl.ds((part * 2 + coil) * 32, 32), lanes]
         return rows.reshape(half, -1).astype(f32)
-
-    first_lane = lax.broadcasted_iota(jnp.int32, (half, 128), 1) == 0
-    for coil in range(2):
-        for block in range(2):
-            rows = pl.ds(block * half, half)
-            for yb in range(2):
-                cols = pl.ds(yb * half, half)
-                dir_re, dir_im = (
-                    rows_s[part, pl.ds(block * 8, 8), :, :, cols].reshape(half, half).astype(f32) for part in range(2)
-                )
-                sens_re, sens_im = (sens(coil, part, block, cols) for part in range(2))
-                image_s[coil, 0, rows, cols] = (sens_re * dir_re - sens_im * dir_im).astype(bf16)
-                image_s[coil, 1, rows, cols] = (sens_re * dir_im + sens_im * dir_re).astype(bf16)
-            from_re = dot(image_s[coil, 0, rows, :], fold_ref[...])
-            from_im = dot(image_s[coil, 1, rows, :], fold_ref[...])
-            re_cos, re_sin = from_re[:, :half], from_re[:, half:]
-            im_cos, im_sin = from_im[:, :half], from_im[:, half:]
-            low = (re_cos + im_sin, im_cos - re_sin)
-            high = (re_cos - im_sin, im_cos + re_sin)
-            low_first = (re_cos, im_cos)
-            high_first = (re_sin, im_sin)
-            for part in range(2):
-                for start, value, first in ((0, low[part], low_first[part]), (half, high[part], high_first[part])):
-                    spec_s[coil, part, rows, pl.ds(start, 128)] = jnp.where(
-                        first_lane, first[:, :128], value[:, :128]
-                    ).astype(bf16)
-                    spec_s[coil, part, rows, pl.ds(start + 128, 128)] = value[:, 128:].astype(bf16)
 
     first_row = lax.broadcasted_iota(jnp.int32, (128, half), 0) == 0
     for coil in range(2):
         for nb in range(2):
             cols = pl.ds(nb * half, half)
-            from_re = dot(fold_t_ref[...], spec_s[coil, 0, :, cols])
-            from_im = dot(fold_t_ref[...], spec_s[coil, 1, :, cols])
+            from_re = dot(fold_t_ref[...], spec_s[coil, 0, :, :, :, cols].reshape(size, half))
+            from_im = dot(fold_t_ref[...], spec_s[coil, 1, :, :, :, cols].reshape(size, half))
 
             def kept(group):
                 rows = slice(group * 128, group * 128 + 128)
@@ -213,13 +260,13 @@
                 send_ref[slabs, yb * 2 + lb] = jnp.where(core == 0, odd, even).reshape(8, 32, 128)
 
 
-def operator(coil, got, mate, fold_tabs, direction, residual, image):
+def operator(coil, got, mate, ready, fold_tabs, direction, residual, image):
     hbm = pl.BlockSpec(memory_space=pltpu.HBM)
     smem = pl.BlockSpec(memory_space=pltpu.SMEM)
     vmem = pl.BlockSpec(memory_space=pltpu.VMEM)
     return pl.pallas_call(
         operator_kernel,
-        in_specs=[smem] + [vmem] * 10 + [hbm] * 3,
+        in_specs=[smem] + [vmem] * 11 + [hbm] * 3,
         out_specs=[vmem] * 3,
         out_shape=[
             jax.ShapeDtypeStruct((16, 4, 32, 128), jnp.float32),
@@ -227,18 +274,18 @@
             jax.ShapeDtypeStruct((3, 8, 32, 128), jnp.float32),
         ],
         scratch_shapes=[
-            pltpu.VMEM((2, 2, 512, 512), jnp.bfloat16),
-            pltpu.VMEM((2, 2, 512, 512), jnp.bfloat16),
+            pltpu.VMEM((2, 2, 256, 512), jnp.bfloat16),
+            pltpu.VMEM((2, 2, 16, 2, 16, 512), jnp.bfloat16),
             pltpu.VMEM((2, 512, 512), jnp.bfloat16),
             pltpu.VMEM((2, 512, 512), jnp.bfloat16),
-            pltpu.VMEM((3, 16, 2, 16, 512), jnp.bfloat16),
+            pltpu.VMEM((16, 2, 16, 512), jnp.bfloat16),
             pltpu.VMEM((512, 512), jnp.float32),
             pltpu.VMEM((3, 2, 8, 32, 128), jnp.float32),
             pltpu.SemaphoreType.DMA((3,)),
         ],
         compiler_params=pltpu.CompilerParams(vmem_limit_bytes=32 * 1024 * 1024),
         name="operator",
-    )(coil, got, mate, *fold_tabs, direction, residual, image)
+    )(coil, got, mate, ready, *fold_tabs, direction, residual, image)
 
 
 def sums_kernel(part_ref, own_ref, applied_ref, sums_ref):
@@ -293,7 +340,8 @@
     packed = pack(coil % 2, sensitivity, direction, sampling.T)
     got = lax.all_to_all(packed.reshape(16, 176, 512), "space", 0, 0, tiled=True)
     mate = lax.ppermute(got[:, 128:], "coil", mates)
-    keep, send, own = operator(coil, got, mate, fold_tabs, direction, residual, image)
+    ready = own_rows(coil, got, fold_tabs[0])
+    keep, send, own = operator(coil, got, mate, ready, fold_tabs, direction, residual, image)
     pair_sum = (keep + lax.ppermute(send, "coil", mates)).astype(jnp.bfloat16)
     parts = lax.all_to_all(
         pair_sum.reshape(64, 32, 128), ("coil", "space"), 0, 0, axis_index_groups=same_core, tiled=True

time: 98.3 us -> 97.1 us (0.988)
    pallas_call x1 -> x2, Pallas kernels: 7.77 us -> 8.1 us  [the longest x1 7.15 us: operator(): pl.pallas_call(operator_kernel, in_specs=[smem] + [vmem] * 11 + [hbm] * 3...]
  transfers between devices with their start and end apart: 2 -> 2, of which waited for: 2 -> 2; matrix products, arithmetic and copies ran while one was open for 0% -> 0% of each run, Pallas kernels for 0% -> 1%
where the time goes in v2:
time: 97.1 us; the launch traced here: 96.8 us
  blocking collectives  77.7 us (80%)
  Pallas kernels  12.3 us (13%)
  waiting for transfers between devices  3.24 us (3%)
  starting transfers between devices  2.37 us (2%)
    all_to_all x1, blocking collectives, on_device(): lax.all_to_all(packed.reshape(16, 176, 512), 'space', 0, 0, tiled=True)  44.5 us
    all_to_all x1, blocking collectives, on_device(): lax.all_to_all(pair_sum.reshape(64, 32, 128), ('coil', 'space'), 0, 0, ax...  18.4 us
    all_to_all x1, blocking collectives, on_device(): lax.all_to_all(sums, ('space', 'coil'), split_axis=0, concat_axis=0, tile...  14.8 us
    pallas_call x1, Pallas kernels, operator(): pl.pallas_call(operator_kernel, in_specs=[smem] + [vmem] * 11 + [hbm] * 3...  7.15 us
    pallas_call x1, Pallas kernels, pack(): pl.pallas_call(pack_kernel, in_specs=[pl.BlockSpec(memory_space=pltpu.SME...  2.82 us
    ppermute x1, waiting for transfers between devices, on_device(): pair_sum = (keep + lax.ppermute(send, 'coil', mates)).astype(jnp.bfloat16)  2.29 us
  transfers between devices with their start and end apart: 2, of which 2 were waited for; matrix products, arithmetic and copies ran while one was open for 0% of the time, Pallas kernels for 1%

profile of v2, /device:TPU:1, one launch (start us, length us, event | category | flops | bytes accessed | tf_op | source)
XLA Modules:
  0.0 96.8 jit_solution(10200705858268852330)
XLA Ops:
  0.6 2.8 %pack.1 = bf16[8,2,176,512]{3,2,1,0:T(8,128)(2,1)} custom-call(s32[1]{0:T(128)S(6)} %select_n.7.core_ref, bf16[2,4,8,32,512]{4,3,2,1,0:T(8,128)(2,1)} %sens_ref.1, f32[2,8,32,512]{3,2,1,0:T(8,128)} %dir_ref.3, s32[32,512]{1,0:T(8,128)} %bitcast.14), custom_call_target="tpu_custom_call" | custom-call | tf_op jit(solution)/shard_map/pack/pallas_call | solution.py:88
  3.5 0.0 copy-start.1
  3.5 0.0 copy-start.9
  3.5 0.0 copy-start.10
  3.5 44.5 %all_to_all.21.got_ref = bf16[16,176,512]{2,1,0:T(8,128)(2,1)S(1)} all-to-all(bf16[16,176,512]{2,1,0:T(8,128)(2,1)} %bitcast.12), channel_id=1, replica_groups=mesh['coil'=8,'space'=16] {'space'}, dimensions={0} | all-to-all | bytes 5767168 | tf_op jit(solution)/shard_map/all_to_all | solution.py:341
  48.1 0.0 copy-start.5
  48.1 0.0 copy-start.6
  48.1 0.0 copy-start.7
  48.1 0.0 copy-start.8
  48.1 0.1 slice.4
  48.2 1.9 %collective-permute-start = (bf16[16,48,512]{2,1,0:T(8,128)(2,1)S(1)}, bf16[16,48,512]{2,1,0:T(8,128)(2,1)S(1)}, u32[]{:S(2)}, u32[]{:S(2)}) collective-permute-start(bf16[16,48,512]{2,1,0:T(8,128)(2,1)S(1)} %slice.4), channel_id=1, source_target_pairs={{0,16},{16,0},{32,48},{48,32},{64,80},{80,64},{96,112},{112,96},{1... | collective-permute-start | bytes 2359304 | tf_op jit(solution)/shard_map/ppermute | solution.py:342
  50.1 0.0 copy-done.1
  50.1 0.9 own_rows.1.ready_ref
  51.0 1.0 collective-permute-done.mate_ref
  52.0 0.0 copy-done.9
  52.0 0.0 copy-done.10
  52.0 0.0 copy-done
  52.0 0.0 copy-done.2
  52.0 0.0 copy-done.3
  52.0 0.0 copy-done.4
  52.0 0.0 copy-done.5
  52.0 0.0 copy-done.6
  52.0 0.0 copy-done.7
  52.0 0.0 copy-done.8
  52.0 7.2 %operator.1 = (f32[16,4,32,128]{3,2,1,0:T(8,128)S(1)}, f32[16,4,32,128]{3,2,1,0:T(8,128)S(1)}, f32[3,8,32,128]{3,2,1,0:T(8,128)S(1)}) custom-call(s32[1]{0:T(128)} %bitcast.coil_ref, bf16[16,176,512]{2,1,0:T(8,128)(2,1)S(1)} %all_to_all.21.got_ref, bf16[16,48,512]{2,1,0:T(8,128)(2,1)S(1)} %collective-permute-done.mate_ref, ...), custom_call_target="tpu_custom_call" | custom-call | tf_op jit(solution)/shard_map/operator/pallas_call | solution.py:267
  59.2 0.5 collective-permute-start.1
  59.7 2.3 %collective-permute-done.1 = f32[16,4,32,128]{3,2,1,0:T(8,128)S(1)} collective-permute-done((f32[16,4,32,128]{3,2,1,0:T(8,128)S(1)}, f32[16,4,32,128]{3,2,1,0:T(8,128)S(1)}, u32[]{:S(2)}, u32[]{:S(2)}) %collective-permute-start.1) | collective-permute-done | bytes 1048608 | tf_op jit(solution)/shard_map/ppermute | solution.py:345
  62.0 0.2 add_convert_fusion
  62.2 18.4 %all_to_all.22 = bf16[64,32,128]{2,1,0:T(8,128)(2,1)S(1)} all-to-all(bf16[64,32,128]{2,1,0:T(8,128)(2,1)S(1)} %bitcast.13), channel_id=1, replica_groups={{0,32,64,96,1,33,65,97,2,34,66,98,3,35,67,99,4,36,68,100,5,37,69,101,6,..., dimensions={0} | all-to-all | bytes 1048576 | tf_op jit(solution)/shard_map/all_to_all | solution.py:346
  80.6 0.3 sums.1
  80.9 14.8 %all_to_all.23 = f32[128,1,128]{2,1,0:T(1,128)S(1)} all-to-all(f32[128,1,128]{2,1,0:T(1,128)S(1)} %bitcast.11), channel_id=1, replica_groups=mesh['coil'=8,'space'=16] {'space','coil'}, dimensions={0} | all-to-all | bytes 131072 | tf_op jit(solution)/shard_map/all_to_all | solution.py:362
  95.7 1.1 %final.1 = (f32[2,8,32,64]{3,2,1,0:T(8,128)}, f32[2,8,32,64]{3,2,1,0:T(8,128)}, f32[2,8,32,64]{3,2,1,0:T(8,128)}) custom-call(f32[128,128]{1,0:T(8,128)S(1)} %bitcast.10, f32[8,32,128]{2,1,0:T(8,128)S(1)} %get-tuple-element.12.applied_ref, f32[3,8,32,128]{3,2,1,0:T(8,128)S(1)} %get-tuple-element.10.own_ref), custom_call_target="tpu_custom_call" | custom-call | tf_op jit(solution)/shard_map/final/pallas_call | solution.py:363
  (4 shorter events, 0.0 us)
Async XLA Ops:
  3.5 46.6 %copy-start.1 = (bf16[512,512]{1,0:T(8,128)(2,1)S(1)}, bf16[512,512]{1,0:T(8,128)(2,1)}, u32[]{:S(2)}) copy-start(bf16[512,512]{1,0:T(8,128)(2,1)} %constant.41.clone.fold_ref) | copy-start | bytes 1572868
  3.5 48.5 %copy-start.9 = (bf16[512,512]{1,0:T(8,128)(2,1)S(1)}, bf16[512,512]{1,0:T(8,128)(2,1)}, u32[]{:S(2)}) copy-start(bf16[512,512]{1,0:T(8,128)(2,1)} %constant.43.clone.pick_ref) | copy-start | bytes 1572868
  3.5 48.5 %copy-start.10 = (bf16[512,512]{1,0:T(8,128)(2,1)S(1)}, bf16[512,512]{1,0:T(8,128)(2,1)}, u32[]{:S(2)}) copy-start(bf16[512,512]{1,0:T(8,128)(2,1)} %constant.42.clone.fold_t_ref) | copy-start | bytes 1572868
  48.1 3.9 %copy-start = (f32[2,8,32,512]{3,2,1,0:T(8,128)S(1)}, f32[2,8,32,512]{3,2,1,0:T(8,128)}, u32[]{:S(2)}) copy-start(f32[2,8,32,512]{3,2,1,0:T(8,128)} %dir_ref.3) | copy-start | bytes 3145732
  48.1 3.9 %copy-start.2 = (f32[2,8,32,512]{3,2,1,0:T(8,128)S(1)}, f32[2,8,32,512]{3,2,1,0:T(8,128)}, u32[]{:S(2)}) copy-start(f32[2,8,32,512]{3,2,1,0:T(8,128)} %res_ref.1) | copy-start | bytes 3145732
  48.1 3.9 %copy-start.3 = (f32[2,8,32,512]{3,2,1,0:T(8,128)S(1)}, f32[2,8,32,512]{3,2,1,0:T(8,128)}, u32[]{:S(2)}) copy-start(f32[2,8,32,512]{3,2,1,0:T(8,128)} %img_ref.1) | copy-start | bytes 3145732
  48.1 3.9 %copy-start.4 = (bf16[512,512]{1,0:T(8,128)(2,1)S(1)}, bf16[512,512]{1,0:T(8,128)(2,1)}, u32[]{:S(2)}) copy-start(bf16[512,512]{1,0:T(8,128)(2,1)} %constant.48.clone.y_odd_ref) | copy-start | bytes 1572868
  48.1 3.9 %copy-start.5 = (bf16[512,512]{1,0:T(8,128)(2,1)S(1)}, bf16[512,512]{1,0:T(8,128)(2,1)}, u32[]{:S(2)}) copy-start(bf16[512,512]{1,0:T(8,128)(2,1)} %constant.47.clone.z_odd_ref) | copy-start | bytes 1572868
  48.1 3.9 %copy-start.6 = (bf16[512,512]{1,0:T(8,128)(2,1)S(1)}, bf16[512,512]{1,0:T(8,128)(2,1)}, u32[]{:S(2)}) copy-start(bf16[512,512]{1,0:T(8,128)(2,1)} %constant.46.clone.y_even_ref) | copy-start | bytes 1572868
  48.1 3.9 %copy-start.7 = (bf16[512,512]{1,0:T(8,128)(2,1)S(1)}, bf16[512,512]{1,0:T(8,128)(2,1)}, u32[]{:S(2)}) copy-start(bf16[512,512]{1,0:T(8,128)(2,1)} %constant.45.clone.z_even_ref) | copy-start | bytes 1572868
  48.1 3.9 %copy-start.8 = (bf16[512,512]{1,0:T(8,128)(2,1)S(1)}, bf16[512,512]{1,0:T(8,128)(2,1)}, u32[]{:S(2)}) copy-start(bf16[512,512]{1,0:T(8,128)(2,1)} %constant.44.clone.pick_t_ref) | copy-start | bytes 1572868
  48.2 3.8 %collective-permute-start = (bf16[16,48,512]{2,1,0:T(8,128)(2,1)S(1)}, bf16[16,48,512]{2,1,0:T(8,128)(2,1)S(1)}, u32[]{:S(2)}, u32[]{:S(2)}) collective-permute-start(bf16[16,48,512]{2,1,0:T(8,128)(2,1)S(1)} %slice.4), channel_id=1, source_target_pairs={{0,16},{16,0},{32,48},{48,32},{64,80},{80,64},{96,112},{112,96},{1... | collective-permute-start | bytes 2359304 | tf_op jit(solution)/shard_map/ppermute | solution.py:342
  59.2 2.8 %collective-permute-start.1 = (f32[16,4,32,128]{3,2,1,0:T(8,128)S(1)}, f32[16,4,32,128]{3,2,1,0:T(8,128)S(1)}, u32[]{:S(2)}, u32[]{:S(2)}) collective-permute-start(f32[16,4,32,128]{3,2,1,0:T(8,128)S(1)} %get-tuple-element.9), channel_id=1, source_target_pairs={{0,16},{16,0},{32,48},{48,32},{64,80},{80,64},{96,112},{112,96},{1... | collective-permute-start | bytes 3145736 | tf_op jit(solution)/shard_map/ppermute | solution.py:345

commit v3 on v2

--- a/solution.py
+++ b/solution.py
@@ -122,6 +122,7 @@
             )
             image_s[coil, 0, :, cols] = (sens_re * dir_re - sens_im * dir_im).astype(jnp.bfloat16)
             image_s[coil, 1, :, cols] = (sens_re * dir_im + sens_im * dir_re).astype(jnp.bfloat16)
+    for coil in range(2):
         from_re = dot(image_s[coil, 0], fold_ref[...])
         from_im = dot(image_s[coil, 1], fold_ref[...])
         re_cos, re_sin = from_re[:, :half], from_re[:, half:]
@@ -137,37 +138,9 @@
                 store(coil, part, start + 128, value[:, 128:].astype(jnp.bfloat16))
 
 
-def own_rows_kernel(coil_ref, got_ref, fold_ref, out_ref, image_s):
-    def store(coil, part, start, value):
-        out_ref[coil, part, :, :, pl.ds(start, 128)] = value.reshape(16, 16, 128)
-
-    dir_parts = [got_ref.at[:, pl.ds(128 + part * 16, 16), :] for part in range(2)]
-    spectrum_rows(got_ref, dir_parts, coil_ref[0] % 2, fold_ref, image_s, store)
-
-
-def own_rows(coil, got, fold):
-    vmem = pl.BlockSpec(memory_space=pltpu.VMEM)
-    return pl.pallas_call(
-        own_rows_kernel,
-        in_specs=[pl.BlockSpec(memory_space=pltpu.SMEM), vmem, vmem],
-        out_specs=vmem,
-        out_shape=jax.ShapeDtypeStruct((2, 2, 16, 16, 512), jnp.bfloat16),
-        scratch_shapes=[pltpu.VMEM((2, 2, 256, 512), jnp.bfloat16)],
-        compiler_params=pltpu.CompilerParams(vmem_limit_bytes=16 * 1024 * 1024),
-        name="own_rows",
-    )(coil, got, fold)
-
-
-def operator_kernel(
-    coil_ref, got_ref, mate_ref, ready_ref, fold_ref, fold_t_ref, pick_ref, pick_t_ref,
-    z_even_ref, y_even_ref, z_odd_ref, y_odd_ref, dir_ref, res_ref, img_ref,
-    keep_ref, send_ref, own_ref,
-    image_s, spec_s, even_s, odd_s, mask_t_s, mask_s, own_s, sems,
+def own_rows_kernel(
+    coil_ref, got_ref, fold_ref, pick_ref, dir_ref, res_ref, img_ref, out_ref, mask_ref, own_ref, image_s, own_s, sems
 ):
-    size = 512
-    half = 256
-    f32 = jnp.float32
-    bf16 = jnp.bfloat16
     core = coil_ref[0] % 2
     own_lanes = pl.ds(pl.multiple_of(coil_ref[0] // 2 * 128, 128), 128)
     own_copies = [
@@ -177,11 +150,62 @@
     for copy in own_copies:
         copy.start()
 
-    mask_t_s[:, core] = got_ref[:, pl.ds(160, 16), :]
-    mask_t_s[:, 1 - core] = mate_ref[:, pl.ds(32, 16), :]
-    mask_t = dot(pick_t_ref[...], mask_t_s[...].reshape(size, size)).astype(bf16)
-    mask_s[...] = dot(mask_t, pick_ref[...]).T
-
+    def store(coil, part, start, value):
+        out_ref[coil, part, :, :, pl.ds(start, 128)] = value.reshape(16, 16, 128)
+
+    dir_parts = [got_ref.at[:, pl.ds(128 + part * 16, 16), :] for part in range(2)]
+    spectrum_rows(got_ref, dir_parts, core, fold_ref, image_s, store)
+    mask_ref[...] = mask_columns(got_ref[:, pl.ds(160, 16), :], pick_ref)
+    for copy in own_copies:
+        copy.wait()
+    for index in range(3):
+        even, odd = paired(*(own_s[index, part].reshape(256, 128) for part in range(2)))
+        own_ref[index] = jnp.where(core == 0, even, odd).reshape(8, 32, 128)
+
+
+def mask_columns(rows, pick_ref):
+    return dot(rows.reshape(256, 512), pick_ref[...]).astype(jnp.bfloat16).reshape(16, 16, 512)
+
+
+def paired(re, im):
+    lower = lax.broadcasted_iota(jnp.int32, re.shape, 1) < 64
+    moved = pltpu.roll(jnp.where(lower, im, re), 64, 1)
+    return jnp.where(lower, re, moved), jnp.where(lower, moved, im)
+
+
+def own_rows(coil, got, fold, pick, direction, residual, image):
+    hbm = pl.BlockSpec(memory_space=pltpu.HBM)
+    vmem = pl.BlockSpec(memory_space=pltpu.VMEM)
+    return pl.pallas_call(
+        own_rows_kernel,
+        in_specs=[pl.BlockSpec(memory_space=pltpu.SMEM)] + [vmem] * 3 + [hbm] * 3,
+        out_specs=[vmem] * 3,
+        out_shape=[
+            jax.ShapeDtypeStruct((2, 2, 16, 16, 512), jnp.bfloat16),
+            jax.ShapeDtypeStruct((16, 16, 512), jnp.bfloat16),
+            jax.ShapeDtypeStruct((3, 8, 32, 128), jnp.float32),
+        ],
+        scratch_shapes=[
+            pltpu.VMEM((2, 2, 256, 512), jnp.bfloat16),
+            pltpu.VMEM((3, 2, 8, 32, 128), jnp.float32),
+            pltpu.SemaphoreType.DMA((3,)),
+        ],
+        compiler_params=pltpu.CompilerParams(vmem_limit_bytes=16 * 1024 * 1024),
+        name="own_rows",
+    )(coil, got, fold, pick, direction, residual, image)
+
+
+def operator_kernel(
+    coil_ref, got_ref, mate_ref, ready_ref, mask_ref, fold_ref, fold_t_ref, pick_ref, pick_t_ref,
+    z_even_ref, y_even_ref, z_odd_ref, y_odd_ref,
+    keep_ref, send_ref,
+    image_s, spec_s, even_s, odd_s, mask_t_s, mask_s,
+):
+    size = 512
+    half = 256
+    f32 = jnp.float32
+    bf16 = jnp.bfloat16
+    core = coil_ref[0] % 2
     def store(coil, part, start, value):
         spec_s[coil, part, :, 1 - core, :, pl.ds(start, 128)] = value.reshape(16, 16, 128)
 
@@ -191,16 +215,22 @@
         for part in range(2):
             spec_s[coil, part, :, core] = ready_ref[coil, part]
 
+    mask_t_s[:, core] = mask_ref[...]
+    mask_t_s[:, 1 - core] = mask_columns(mate_ref[:, pl.ds(32, 16), :], pick_ref)
+    mask_s[...] = dot(pick_t_ref[...], mask_t_s[...].reshape(size, size)).T
+
     def sens(coil, part, block, lanes):
         rows = got_ref[pl.ds(block * 8, 8), pl.ds((part * 2 + coil) * 32, 32), lanes]
         return rows.reshape(half, -1).astype(f32)
 
     first_row = lax.broadcasted_iota(jnp.int32, (128, half), 0) == 0
     for coil in range(2):
+        full_re = dot(fold_t_ref[...], spec_s[coil, 0].reshape(size, size))
+        full_im = dot(fold_t_ref[...], spec_s[coil, 1].reshape(size, size))
         for nb in range(2):
             cols = pl.ds(nb * half, half)
-            from_re = dot(fold_t_ref[...], spec_s[coil, 0, :, :, :, cols].reshape(size, half))
-            from_im = dot(fold_t_ref[...], spec_s[coil, 1, :, :, :, cols].reshape(size, half))
+            from_re = full_re[:, nb * half : nb * half + half]
+            from_im = full_im[:, nb * half : nb * half + half]
 
             def kept(group):
                 rows = slice(group * 128, group * 128 + 128)
@@ -225,19 +255,6 @@
                 for block in range(2):
                     even_s[coil, pl.ds(block * half, half), at] = back[block][:, :128]
                     odd_s[coil, pl.ds(block * half, half), at] = back[block][:, 128:]
-
-    for copy in own_copies:
-        copy.wait()
-    lower = lax.broadcasted_iota(jnp.int32, (half, 128), 1) < 64
-
-    def paired(re, im):
-        even = jnp.where(lower, re, pltpu.roll(im, 64, 1))
-        odd = jnp.where(lower, pltpu.roll(re, 64, 1), im)
-        return even, odd
-
-    for index in range(3):
-        even, odd = paired(*(own_s[index, part].reshape(half, 128) for part in range(2)))
-        own_ref[index] = jnp.where(core == 0, even, odd).reshape(8, 32, 128)
 
     for block in range(2):
         rows = pl.ds(block * half, half)
@@ -257,21 +274,19 @@
                 even, odd = paired(sums[yb][0][:, lanes], sums[yb][1][:, lanes])
                 slabs = pl.ds(block * 8, 8)
                 keep_ref[slabs, yb * 2 + lb] = jnp.where(core == 0, even, odd).reshape(8, 32, 128)
-                send_ref[slabs, yb * 2 + lb] = jnp.where(core == 0, odd, even).reshape(8, 32, 128)
-
-
-def operator(coil, got, mate, ready, fold_tabs, direction, residual, image):
-    hbm = pl.BlockSpec(memory_space=pltpu.HBM)
+                send_ref[slabs, yb * 2 + lb] = jnp.where(core == 0, odd, even).reshape(8, 32, 128).astype(bf16)
+
+
+def operator(coil, got, mate, ready, mask, fold_tabs):
     smem = pl.BlockSpec(memory_space=pltpu.SMEM)
     vmem = pl.BlockSpec(memory_space=pltpu.VMEM)
     return pl.pallas_call(
         operator_kernel,
-        in_specs=[smem] + [vmem] * 11 + [hbm] * 3,
-        out_specs=[vmem] * 3,
+        in_specs=[smem] + [vmem] * 12,
+        out_specs=[vmem] * 2,
         out_shape=[
             jax.ShapeDtypeStruct((16, 4, 32, 128), jnp.float32),
-            jax.ShapeDtypeStruct((16, 4, 32, 128), jnp.float32),
-            jax.ShapeDtypeStruct((3, 8, 32, 128), jnp.float32),
+            jax.ShapeDtypeStruct((16, 4, 32, 128), jnp.bfloat16),
         ],
         scratch_shapes=[
             pltpu.VMEM((2, 2, 256, 512), jnp.bfloat16),
@@ -280,12 +295,10 @@
             pltpu.VMEM((2, 512, 512), jnp.bfloat16),
             pltpu.VMEM((16, 2, 16, 512), jnp.bfloat16),
             pltpu.VMEM((512, 512), jnp.float32),
-            pltpu.VMEM((3, 2, 8, 32, 128), jnp.float32),
-            pltpu.SemaphoreType.DMA((3,)),
         ],
         compiler_params=pltpu.CompilerParams(vmem_limit_bytes=32 * 1024 * 1024),
         name="operator",
-    )(coil, got, mate, ready, *fold_tabs, direction, residual, image)
+    )(coil, got, mate, ready, mask, *fold_tabs)
 
 
 def sums_kernel(part_ref, own_ref, applied_ref, sums_ref):
@@ -340,8 +353,8 @@
     packed = pack(coil % 2, sensitivity, direction, sampling.T)
     got = lax.all_to_all(packed.reshape(16, 176, 512), "space", 0, 0, tiled=True)
     mate = lax.ppermute(got[:, 128:], "coil", mates)
-    ready = own_rows(coil, got, fold_tabs[0])
-    keep, send, own = operator(coil, got, mate, ready, fold_tabs, direction, residual, image)
+    ready, mask, own = own_rows(coil, got, fold_tabs[0], fold_tabs[2], direction, residual, image)
+    keep, send = operator(coil, got, mate, ready, mask, fold_tabs)
     pair_sum = (keep + lax.ppermute(send, "coil", mates)).astype(jnp.bfloat16)
     parts = lax.all_to_all(
         pair_sum.reshape(64, 32, 128), ("coil", "space"), 0, 0, axis_index_groups=same_core, tiled=True

time: 97.1 us -> 95.6 us (0.985)
  waiting for transfers between devices: 3.24 us -> 2.04 us
where the time goes in v3:
time: 95.6 us; the launch traced here: 95.3 us
  blocking collectives  77.9 us (81%)
  Pallas kernels  12 us (13%)
  starting transfers between devices  2.34 us (2%)
  waiting for transfers between devices  2.04 us (2%)
    all_to_all x1, blocking collectives, on_device(): lax.all_to_all(packed.reshape(16, 176, 512), 'space', 0, 0, tiled=True)  44.7 us
    all_to_all x1, blocking collectives, on_device(): lax.all_to_all(pair_sum.reshape(64, 32, 128), ('coil', 'space'), 0, 0, ax...  18.4 us
    all_to_all x1, blocking collectives, on_device(): lax.all_to_all(sums, ('space', 'coil'), split_axis=0, concat_axis=0, tile...  14.8 us
    pallas_call x1, Pallas kernels, operator(): pl.pallas_call(operator_kernel, in_specs=[smem] + [vmem] * 12, out_specs=...  6.39 us
    pallas_call x1, Pallas kernels, pack(): pl.pallas_call(pack_kernel, in_specs=[pl.BlockSpec(memory_space=pltpu.SME...  2.83 us
  transfers between devices with their start and end apart: 2, of which 2 were waited for; matrix products, arithmetic and copies ran while one was open for 0% of the time, Pallas kernels for 1%

profile of v3, /device:TPU:1, one launch (start us, length us, event | category | flops | bytes accessed | tf_op | source)
XLA Modules:
  0.0 95.3 jit_solution(9827402221704199364)
XLA Ops:
  0.6 2.8 %pack.1 = bf16[8,2,176,512]{3,2,1,0:T(8,128)(2,1)} custom-call(s32[1]{0:T(128)S(6)} %select_n.7.core_ref, bf16[2,4,8,32,512]{4,3,2,1,0:T(8,128)(2,1)} %sens_ref.1, f32[2,8,32,512]{3,2,1,0:T(8,128)} %dir_ref.3, s32[32,512]{1,0:T(8,128)} %bitcast.14), custom_call_target="tpu_custom_call" | custom-call | tf_op jit(solution)/shard_map/pack/pallas_call | solution.py:88
  3.5 0.0 copy-start
  3.5 0.0 copy-start.1
  3.5 0.0 copy-start.2
  3.5 0.0 copy-start.3
  3.5 0.0 copy-start.4
  3.5 44.7 %all_to_all.21.got_ref = bf16[16,176,512]{2,1,0:T(8,128)(2,1)S(1)} all-to-all(bf16[16,176,512]{2,1,0:T(8,128)(2,1)} %bitcast.12), channel_id=1, replica_groups=mesh['coil'=8,'space'=16] {'space'}, dimensions={0} | all-to-all | bytes 5767168 | tf_op jit(solution)/shard_map/all_to_all | solution.py:354
  48.2 0.1 slice.4
  48.3 0.0 copy-start.5
  48.3 0.0 copy-start.6
  48.3 0.0 copy-start.7
  48.3 0.0 copy-start.8
  48.3 0.0 copy-start.9
  48.3 0.0 copy-start.10
  48.4 1.9 %collective-permute-start = (bf16[16,48,512]{2,1,0:T(8,128)(2,1)S(1)}, bf16[16,48,512]{2,1,0:T(8,128)(2,1)S(1)}, u32[]{:S(2)}, u32[]{:S(2)}) collective-permute-start(bf16[16,48,512]{2,1,0:T(8,128)(2,1)S(1)} %slice.4), channel_id=1, source_target_pairs={{0,16},{16,0},{32,48},{48,32},{64,80},{80,64},{96,112},{112,96},{1... | collective-permute-start | bytes 2359304 | tf_op jit(solution)/shard_map/ppermute | solution.py:355
  50.2 0.0 copy-done
  50.2 0.0 copy-done.1
  50.2 0.0 copy-done.2
  50.2 0.0 copy-done.3
  50.2 0.0 copy-done.4
  50.3 1.4 %own_rows.1 = (bf16[2,2,16,16,512]{4,3,2,1,0:T(8,128)(2,1)S(1)}, bf16[16,16,512]{2,1,0:T(8,128)(2,1)S(1)}, f32[3,8,32,128]{3,2,1,0:T(8,128)S(1)}) custom-call(s32[1]{0:T(128)} %bitcast.coil_ref, bf16[16,176,512]{2,1,0:T(8,128)(2,1)S(1)} %all_to_all.21.got_ref, bf16[512,512]{1,0:T(8,128)(2,1)S(1)} %copy-done.2, bf16[512,512]{1,0:T(8,128)(2,1)S(1)} %copy-done.1, ...), custom_call_target="tpu_custom_call" | custom-call | tf_op jit(solution)/shard_map/own_rows/pallas_call | solution.py:179
  51.6 0.5 collective-permute-done.mate_ref
  52.1 0.0 copy-done.5
  52.1 0.0 copy-done.7
  52.2 6.4 %operator.1 = (f32[16,4,32,128]{3,2,1,0:T(8,128)S(1)}, bf16[16,4,32,128]{3,2,1,0:T(8,128)(2,1)S(1)}) custom-call(s32[1]{0:T(128)} %bitcast.coil_ref, bf16[16,176,512]{2,1,0:T(8,128)(2,1)S(1)} %all_to_all.21.got_ref, bf16[16,48,512]{2,1,0:T(8,128)(2,1)S(1)} %collective-permute-done.mate_ref, bf16[2,2,16,16,512]{4,3,2,1,0:T(8,128)(2,1)S(1)} %get-tuple-element.10.ready_ref, ...), custom_call_target="tpu_custom_call" | custom-call | tf_op jit(solution)/shard_map/operator/pallas_call | solution.py:283
  58.6 0.5 collective-permute-start.1
  59.0 1.5 %collective-permute-done.1 = bf16[16,4,32,128]{3,2,1,0:T(8,128)(2,1)S(1)} collective-permute-done((bf16[16,4,32,128]{3,2,1,0:T(8,128)(2,1)S(1)}, bf16[16,4,32,128]{3,2,1,0:T(8,128)(2,1)S(1)}, u32[]{:S(2)}, u32[]{:S(2)}) %collective-permute-start.1) | collective-permute-done | bytes 524320 | tf_op jit(solution)/shard_map/ppermute | solution.py:358
  60.6 0.2 add_convert_fusion
  60.7 18.4 %all_to_all.22 = bf16[64,32,128]{2,1,0:T(8,128)(2,1)S(1)} all-to-all(bf16[64,32,128]{2,1,0:T(8,128)(2,1)S(1)} %bitcast.13), channel_id=1, replica_groups={{0,32,64,96,1,33,65,97,2,34,66,98,3,35,67,99,4,36,68,100,5,37,69,101,6,..., dimensions={0} | all-to-all | bytes 1048576 | tf_op jit(solution)/shard_map/all_to_all | solution.py:359
  79.1 0.3 sums.1
  79.4 14.8 %all_to_all.23 = f32[128,1,128]{2,1,0:T(1,128)S(1)} all-to-all(f32[128,1,128]{2,1,0:T(1,128)S(1)} %bitcast.11), channel_id=1, replica_groups=mesh['coil'=8,'space'=16] {'space','coil'}, dimensions={0} | all-to-all | bytes 131072 | tf_op jit(solution)/shard_map/all_to_all | solution.py:375
  94.2 1.1 %final.1 = (f32[2,8,32,64]{3,2,1,0:T(8,128)}, f32[2,8,32,64]{3,2,1,0:T(8,128)}, f32[2,8,32,64]{3,2,1,0:T(8,128)}) custom-call(f32[128,128]{1,0:T(8,128)S(1)} %bitcast.10, f32[8,32,128]{2,1,0:T(8,128)S(1)} %get-tuple-element.16.applied_ref, f32[3,8,32,128]{3,2,1,0:T(8,128)S(1)} %get-tuple-element.14.own_ref), custom_call_target="tpu_custom_call" | custom-call | tf_op jit(solution)/shard_map/final/pallas_call | solution.py:376
  (4 shorter events, 0.0 us)
Async XLA Ops:
  3.5 46.7 %copy-start = (f32[2,8,32,512]{3,2,1,0:T(8,128)S(1)}, f32[2,8,32,512]{3,2,1,0:T(8,128)}, u32[]{:S(2)}) copy-start(f32[2,8,32,512]{3,2,1,0:T(8,128)} %dir_ref.3) | copy-start | bytes 3145732
  3.5 46.7 %copy-start.1 = (bf16[512,512]{1,0:T(8,128)(2,1)S(1)}, bf16[512,512]{1,0:T(8,128)(2,1)}, u32[]{:S(2)}) copy-start(bf16[512,512]{1,0:T(8,128)(2,1)} %constant.43.clone.pick_ref) | copy-start | bytes 1572868
  3.5 46.7 %copy-start.2 = (bf16[512,512]{1,0:T(8,128)(2,1)S(1)}, bf16[512,512]{1,0:T(8,128)(2,1)}, u32[]{:S(2)}) copy-start(bf16[512,512]{1,0:T(8,128)(2,1)} %constant.41.clone.fold_ref) | copy-start | bytes 1572868
  3.5 46.7 %copy-start.3 = (f32[2,8,32,512]{3,2,1,0:T(8,128)S(1)}, f32[2,8,32,512]{3,2,1,0:T(8,128)}, u32[]{:S(2)}) copy-start(f32[2,8,32,512]{3,2,1,0:T(8,128)} %res_ref.1) | copy-start | bytes 3145732
  3.5 46.7 %copy-start.4 = (f32[2,8,32,512]{3,2,1,0:T(8,128)S(1)}, f32[2,8,32,512]{3,2,1,0:T(8,128)}, u32[]{:S(2)}) copy-start(f32[2,8,32,512]{3,2,1,0:T(8,128)} %img_ref.1) | copy-start | bytes 3145732
  48.3 3.9 %copy-start.5 = (bf16[512,512]{1,0:T(8,128)(2,1)S(1)}, bf16[512,512]{1,0:T(8,128)(2,1)}, u32[]{:S(2)}) copy-start(bf16[512,512]{1,0:T(8,128)(2,1)} %constant.48.clone.y_odd_ref) | copy-start | bytes 1572868
  48.3 3.9 %copy-start.6 = (bf16[512,512]{1,0:T(8,128)(2,1)S(1)}, bf16[512,512]{1,0:T(8,128)(2,1)}, u32[]{:S(2)}) copy-start(bf16[512,512]{1,0:T(8,128)(2,1)} %constant.47.clone.z_odd_ref) | copy-start | bytes 1572868
  48.3 3.8 %copy-start.7 = (bf16[512,512]{1,0:T(8,128)(2,1)S(1)}, bf16[512,512]{1,0:T(8,128)(2,1)}, u32[]{:S(2)}) copy-start(bf16[512,512]{1,0:T(8,128)(2,1)} %constant.46.clone.y_even_ref) | copy-start | bytes 1572868
  48.3 3.8 %copy-start.8 = (bf16[512,512]{1,0:T(8,128)(2,1)S(1)}, bf16[512,512]{1,0:T(8,128)(2,1)}, u32[]{:S(2)}) copy-start(bf16[512,512]{1,0:T(8,128)(2,1)} %constant.45.clone.z_even_ref) | copy-start | bytes 1572868
  48.3 3.8 %copy-start.9 = (bf16[512,512]{1,0:T(8,128)(2,1)S(1)}, bf16[512,512]{1,0:T(8,128)(2,1)}, u32[]{:S(2)}) copy-start(bf16[512,512]{1,0:T(8,128)(2,1)} %constant.44.clone.pick_t_ref) | copy-start | bytes 1572868
  48.3 3.8 %copy-start.10 = (bf16[512,512]{1,0:T(8,128)(2,1)S(1)}, bf16[512,512]{1,0:T(8,128)(2,1)}, u32[]{:S(2)}) copy-start(bf16[512,512]{1,0:T(8,128)(2,1)} %constant.42.clone.fold_t_ref) | copy-start | bytes 1572868
  48.4 3.8 %collective-permute-start = (bf16[16,48,512]{2,1,0:T(8,128)(2,1)S(1)}, bf16[16,48,512]{2,1,0:T(8,128)(2,1)S(1)}, u32[]{:S(2)}, u32[]{:S(2)}) collective-permute-start(bf16[16,48,512]{2,1,0:T(8,128)(2,1)S(1)} %slice.4), channel_id=1, source_target_pairs={{0,16},{16,0},{32,48},{48,32},{64,80},{80,64},{96,112},{112,96},{1... | collective-permute-start | bytes 2359304 | tf_op jit(solution)/shard_map/ppermute | solution.py:355
  58.6 2.0 %collective-permute-start.1 = (bf16[16,4,32,128]{3,2,1,0:T(8,128)(2,1)S(1)}, bf16[16,4,32,128]{3,2,1,0:T(8,128)(2,1)S(1)}, u32[]{:S(2)}, u32[]{:S(2)}) collective-permute-start(bf16[16,4,32,128]{3,2,1,0:T(8,128)(2,1)S(1)} %get-tuple-element.13), channel_id=1, source_target_pairs={{0,16},{16,0},{32,48},{48,32},{64,80},{80,64},{96,112},{112,96},{1... | collective-permute-start | bytes 1572872 | tf_op jit(solution)/shard_map/ppermute | solution.py:358

commit v4 on v3

--- a/solution.py
+++ b/solution.py
@@ -21,23 +21,36 @@
     return np.cos(phase_angle) * norm_scale, np.sin(phase_angle) * norm_scale
 
 
+QUARTERS = ((0, 0), (2, 3), (1, 1), (3, 2))
+
+
 def fold_tables(length):
     cos_t, sin_t = tables(length)
     half = length // 2
-    even, odd = np.arange(0, half, 2), np.arange(1, half, 2)
-    low = np.concatenate([even, odd])
+    low = np.concatenate([np.arange(rest, half, 4) for rest in (0, 2, 1, 3)])
     high = np.where(low == 0, half, length - low)
     sine = sin_t[:, low].copy()
     sine[:, 0] = cos_t[:, half]
     fold = np.concatenate([cos_t[:, low], sine], axis=1)
-    order = np.concatenate([low, high])
-    pick = np.eye(length, dtype=np.float32)[:, order]
+    pick = np.eye(length, dtype=np.float32)[:, np.concatenate([low, high])]
+
+    def inverse(rows, at):
+        cos_g, sin_g = cos_t[:rows, at], sin_t[:rows, at]
+        return np.block([[cos_g, -sin_g], [sin_g, cos_g]])
+
+    quarter = half // 4
     outs = [fold, fold.T, pick, pick.T]
-    for group in (even, odd):
-        at = np.concatenate([group, np.where(group == 0, half, length - group)])
-        cos_g, sin_g = cos_t[:half, at], sin_t[:half, at]
-        block = np.block([[cos_g, -sin_g], [sin_g, cos_g]])
-        outs += [block, block.T]
+    outs.append(
+        np.stack(
+            [
+                inverse(half // 2, np.concatenate([low[a * quarter :][:quarter], high[b * quarter :][:quarter]]))
+                for a, b in QUARTERS
+            ]
+        )
+    )
+    for start in (0, half // 2):
+        group = slice(start, start + half // 2)
+        outs.append(inverse(half, np.concatenate([low[group], high[group]])).T)
     return [np.ascontiguousarray(out).astype(ml_dtypes.bfloat16) for out in outs]
 
 
@@ -197,7 +210,7 @@
 
 def operator_kernel(
     coil_ref, got_ref, mate_ref, ready_ref, mask_ref, fold_ref, fold_t_ref, pick_ref, pick_t_ref,
-    z_even_ref, y_even_ref, z_odd_ref, y_odd_ref,
+    z_back_ref, y_even_ref, y_odd_ref,
     keep_ref, send_ref,
     image_s, spec_s, even_s, odd_s, mask_t_s, mask_s,
 ):
@@ -223,7 +236,7 @@
         rows = got_ref[pl.ds(block * 8, 8), pl.ds((part * 2 + coil) * 32, 32), lanes]
         return rows.reshape(half, -1).astype(f32)
 
-    first_row = lax.broadcasted_iota(jnp.int32, (128, half), 0) == 0
+    first_row = lax.broadcasted_iota(jnp.int32, (64, half), 0) == 0
     for coil in range(2):
         full_re = dot(fold_t_ref[...], spec_s[coil, 0].reshape(size, size))
         full_im = dot(fold_t_ref[...], spec_s[coil, 1].reshape(size, size))
@@ -232,29 +245,35 @@
             from_re = full_re[:, nb * half : nb * half + half]
             from_im = full_im[:, nb * half : nb * half + half]
 
-            def kept(group):
-                rows = slice(group * 128, group * 128 + 128)
-                rows_2 = slice(half + group * 128, half + group * 128 + 128)
-                re_cos, re_sin = from_re[rows], from_re[rows_2]
-                im_cos, im_sin = from_im[rows], from_im[rows_2]
-                low = [re_cos + im_sin, im_cos - re_sin]
-                high = [re_cos - im_sin, im_cos + re_sin]
-                if group == 0:
-                    low = [jnp.where(first_row, first, value) for first, value in zip((re_cos, im_cos), low)]
-                    high = [jnp.where(first_row, first, value) for first, value in zip((re_sin, im_sin), high)]
-                keep_low, keep_high = mask_s[rows, cols], mask_s[rows_2, cols]
-                pieces = [low[0] * keep_low, high[0] * keep_high, low[1] * keep_low, high[1] * keep_high]
-                return jnp.concatenate([piece.astype(bf16) for piece in pieces], axis=0)
-
-            even = dot(z_even_ref[...], kept(0))
-            odd = dot(z_odd_ref[...], kept(1))
+            def kept(rest):
+                pieces = [[], []]
+                for side, at in enumerate(QUARTERS[rest]):
+                    rows = slice(at * 64, at * 64 + 64)
+                    rows_2 = slice(half + at * 64, half + at * 64 + 64)
+                    re_cos, re_sin = from_re[rows], from_re[rows_2]
+                    im_cos, im_sin = from_im[rows], from_im[rows_2]
+                    if side == 0:
+                        value, first = (re_cos + im_sin, im_cos - re_sin), (re_cos, im_cos)
+                    else:
+                        value, first = (re_cos - im_sin, im_cos + re_sin), (re_sin, im_sin)
+                    keep = mask_s[rows_2 if side else rows, cols]
+                    for part in range(2):
+                        piece = jnp.where(first_row, first[part], value[part]) if at == 0 else value[part]
+                        pieces[part].append((piece * keep).astype(bf16))
+                return jnp.concatenate(pieces[0] + pieces[1], axis=0)
+
+            e0, e1, e2, e3 = (dot(z_back_ref[rest], kept(rest)) for rest in range(4))
+            sum_02, dif_02, sum_13, dif_13 = e0 + e2, e0 - e2, e1 + e3, e1 - e3
+            turned = (dif_02[:128] - dif_13[128:], dif_02[128:] + dif_13[:128])
+            turned_back = (dif_02[:128] + dif_13[128:], dif_02[128:] - dif_13[:128])
+            plus, minus = sum_02 + sum_13, sum_02 - sum_13
+            quarters = ((plus[:128], plus[128:]), turned, (minus[:128], minus[128:]), turned_back)
             for part in range(2):
-                rows = slice(part * half, part * half + half)
-                back = ((even[rows] + odd[rows]).astype(bf16), (even[rows] - odd[rows]).astype(bf16))
                 at = pl.ds(part * half + nb * 128, 128)
-                for block in range(2):
-                    even_s[coil, pl.ds(block * half, half), at] = back[block][:, :128]
-                    odd_s[coil, pl.ds(block * half, half), at] = back[block][:, 128:]
+                for block in range(4):
+                    back = quarters[block][part].astype(bf16)
+                    even_s[coil, pl.ds(block * 128, 128), at] = back[:, :128]
+                    odd_s[coil, pl.ds(block * 128, 128), at] = back[:, 128:]
 
     for block in range(2):
         rows = pl.ds(block * half, half)
@@ -282,7 +301,7 @@
     vmem = pl.BlockSpec(memory_space=pltpu.VMEM)
     return pl.pallas_call(
         operator_kernel,
-        in_specs=[smem] + [vmem] * 12,
+        in_specs=[smem] + [vmem] * 11,
         out_specs=[vmem] * 2,
         out_shape=[
             jax.ShapeDtypeStruct((16, 4, 32, 128), jnp.float32),

time: 95.6 us -> 95.1 us (level)
  no operation moved by 1% of the time
where the time goes in v4:
time: 95.1 us; the launch traced here: 94.9 us
  blocking collectives  77.9 us (82%)
  Pallas kernels  11.6 us (12%)
  starting transfers between devices  2.34 us (2%)
  waiting for transfers between devices  2.03 us (2%)
    all_to_all x1, blocking collectives, on_device(): lax.all_to_all(packed.reshape(16, 176, 512), 'space', 0, 0, tiled=True)  44.7 us
    all_to_all x1, blocking collectives, on_device(): lax.all_to_all(pair_sum.reshape(64, 32, 128), ('coil', 'space'), 0, 0, ax...  18.4 us
    all_to_all x1, blocking collectives, on_device(): lax.all_to_all(sums, ('space', 'coil'), split_axis=0, concat_axis=0, tile...  14.8 us
    pallas_call x1, Pallas kernels, operator(): pl.pallas_call(operator_kernel, in_specs=[smem] + [vmem] * 11, out_specs=...  5.96 us
    pallas_call x1, Pallas kernels, pack(): pl.pallas_call(pack_kernel, in_specs=[pl.BlockSpec(memory_space=pltpu.SME...  2.82 us
  transfers between devices with their start and end apart: 2, of which 2 were waited for; matrix products, arithmetic and copies ran while one was open for 0% of the time, Pallas kernels for 1%

profile of v4, /device:TPU:1, one launch (start us, length us, event | category | flops | bytes accessed | tf_op | source)
XLA Modules:
  0.0 94.9 jit_solution(13101684349573748333)
XLA Ops:
  0.6 2.8 %pack.1 = bf16[8,2,176,512]{3,2,1,0:T(8,128)(2,1)} custom-call(s32[1]{0:T(128)S(6)} %select_n.7.core_ref, bf16[2,4,8,32,512]{4,3,2,1,0:T(8,128)(2,1)} %sens_ref.1, f32[2,8,32,512]{3,2,1,0:T(8,128)} %dir_ref.3, s32[32,512]{1,0:T(8,128)} %bitcast.14), custom_call_target="tpu_custom_call" | custom-call | tf_op jit(solution)/shard_map/pack/pallas_call | solution.py:101
  3.5 0.0 copy-start
  3.5 0.0 copy-start.1
  3.5 0.0 copy-start.2
  3.5 0.0 copy-start.3
  3.5 0.0 copy-start.4
  3.5 44.7 %all_to_all.21.got_ref = bf16[16,176,512]{2,1,0:T(8,128)(2,1)S(1)} all-to-all(bf16[16,176,512]{2,1,0:T(8,128)(2,1)} %bitcast.12), channel_id=1, replica_groups=mesh['coil'=8,'space'=16] {'space'}, dimensions={0} | all-to-all | bytes 5767168 | tf_op jit(solution)/shard_map/all_to_all | solution.py:373
  48.2 0.1 slice.4
  48.3 0.0 copy-start.5
  48.3 0.0 copy-start.6
  48.3 0.0 copy-start.7
  48.3 0.0 copy-start.8
  48.3 0.0 copy-start.9
  48.3 1.9 %collective-permute-start = (bf16[16,48,512]{2,1,0:T(8,128)(2,1)S(1)}, bf16[16,48,512]{2,1,0:T(8,128)(2,1)S(1)}, u32[]{:S(2)}, u32[]{:S(2)}) collective-permute-start(bf16[16,48,512]{2,1,0:T(8,128)(2,1)S(1)} %slice.4), channel_id=1, source_target_pairs={{0,16},{16,0},{32,48},{48,32},{64,80},{80,64},{96,112},{112,96},{1... | collective-permute-start | bytes 2359304 | tf_op jit(solution)/shard_map/ppermute | solution.py:374
  50.2 0.0 copy-done
  50.2 0.0 copy-done.1
  50.2 0.0 copy-done.2
  50.2 0.0 copy-done.3
  50.2 0.0 copy-done.4
  50.2 1.4 %own_rows.1 = (bf16[2,2,16,16,512]{4,3,2,1,0:T(8,128)(2,1)S(1)}, bf16[16,16,512]{2,1,0:T(8,128)(2,1)S(1)}, f32[3,8,32,128]{3,2,1,0:T(8,128)S(1)}) custom-call(s32[1]{0:T(128)} %bitcast.coil_ref, bf16[16,176,512]{2,1,0:T(8,128)(2,1)S(1)} %all_to_all.21.got_ref, bf16[512,512]{1,0:T(8,128)(2,1)S(1)} %copy-done.2, bf16[512,512]{1,0:T(8,128)(2,1)S(1)} %copy-done.1, ...), custom_call_target="tpu_custom_call" | custom-call | tf_op jit(solution)/shard_map/own_rows/pallas_call | solution.py:192
  51.6 0.5 collective-permute-done.mate_ref
  52.1 0.0 copy-done.5
  52.1 0.0 copy-done.6
  52.1 0.0 copy-done.7
  52.1 6.0 %operator.1 = (f32[16,4,32,128]{3,2,1,0:T(8,128)S(1)}, bf16[16,4,32,128]{3,2,1,0:T(8,128)(2,1)S(1)}) custom-call(s32[1]{0:T(128)} %bitcast.coil_ref, bf16[16,176,512]{2,1,0:T(8,128)(2,1)S(1)} %all_to_all.21.got_ref, bf16[16,48,512]{2,1,0:T(8,128)(2,1)S(1)} %collective-permute-done.mate_ref, bf16[2,2,16,16,512]{4,3,2,1,0:T(8,128)(2,1)S(1)} %get-tuple-element.10.ready_ref, ...), custom_call_target="tpu_custom_call" | custom-call | tf_op jit(solution)/shard_map/operator/pallas_call | solution.py:302
  58.1 0.5 collective-permute-start.1
  58.6 1.5 %collective-permute-done.1 = bf16[16,4,32,128]{3,2,1,0:T(8,128)(2,1)S(1)} collective-permute-done((bf16[16,4,32,128]{3,2,1,0:T(8,128)(2,1)S(1)}, bf16[16,4,32,128]{3,2,1,0:T(8,128)(2,1)S(1)}, u32[]{:S(2)}, u32[]{:S(2)}) %collective-permute-start.1) | collective-permute-done | bytes 524320 | tf_op jit(solution)/shard_map/ppermute | solution.py:377
  60.1 0.2 add_convert_fusion
  60.3 18.4 %all_to_all.22 = bf16[64,32,128]{2,1,0:T(8,128)(2,1)S(1)} all-to-all(bf16[64,32,128]{2,1,0:T(8,128)(2,1)S(1)} %bitcast.13), channel_id=1, replica_groups={{0,32,64,96,1,33,65,97,2,34,66,98,3,35,67,99,4,36,68,100,5,37,69,101,6,..., dimensions={0} | all-to-all | bytes 1048576 | tf_op jit(solution)/shard_map/all_to_all | solution.py:378
  78.7 0.3 sums.1
  79.0 14.8 %all_to_all.23 = f32[128,1,128]{2,1,0:T(1,128)S(1)} all-to-all(f32[128,1,128]{2,1,0:T(1,128)S(1)} %bitcast.11), channel_id=1, replica_groups=mesh['coil'=8,'space'=16] {'space','coil'}, dimensions={0} | all-to-all | bytes 131072 | tf_op jit(solution)/shard_map/all_to_all | solution.py:394
  93.8 1.1 %final.1 = (f32[2,8,32,64]{3,2,1,0:T(8,128)}, f32[2,8,32,64]{3,2,1,0:T(8,128)}, f32[2,8,32,64]{3,2,1,0:T(8,128)}) custom-call(f32[128,128]{1,0:T(8,128)S(1)} %bitcast.10, f32[8,32,128]{2,1,0:T(8,128)S(1)} %get-tuple-element.16.applied_ref, f32[3,8,32,128]{3,2,1,0:T(8,128)S(1)} %get-tuple-element.14.own_ref), custom_call_target="tpu_custom_call" | custom-call | tf_op jit(solution)/shard_map/final/pallas_call | solution.py:395
  (2 shorter events, 0.0 us)
Async XLA Ops:
  3.5 46.7 %copy-start = (f32[2,8,32,512]{3,2,1,0:T(8,128)S(1)}, f32[2,8,32,512]{3,2,1,0:T(8,128)}, u32[]{:S(2)}) copy-start(f32[2,8,32,512]{3,2,1,0:T(8,128)} %dir_ref.3) | copy-start | bytes 3145732
  3.5 46.7 %copy-start.1 = (bf16[512,512]{1,0:T(8,128)(2,1)S(1)}, bf16[512,512]{1,0:T(8,128)(2,1)}, u32[]{:S(2)}) copy-start(bf16[512,512]{1,0:T(8,128)(2,1)} %constant.41.clone.pick_ref) | copy-start | bytes 1572868
  3.5 46.7 %copy-start.2 = (bf16[512,512]{1,0:T(8,128)(2,1)S(1)}, bf16[512,512]{1,0:T(8,128)(2,1)}, u32[]{:S(2)}) copy-start(bf16[512,512]{1,0:T(8,128)(2,1)} %constant.39.clone.fold_ref) | copy-start | bytes 1572868
  3.5 46.7 %copy-start.3 = (f32[2,8,32,512]{3,2,1,0:T(8,128)S(1)}, f32[2,8,32,512]{3,2,1,0:T(8,128)}, u32[]{:S(2)}) copy-start(f32[2,8,32,512]{3,2,1,0:T(8,128)} %res_ref.1) | copy-start | bytes 3145732
  3.5 46.7 %copy-start.4 = (f32[2,8,32,512]{3,2,1,0:T(8,128)S(1)}, f32[2,8,32,512]{3,2,1,0:T(8,128)}, u32[]{:S(2)}) copy-start(f32[2,8,32,512]{3,2,1,0:T(8,128)} %img_ref.1) | copy-start | bytes 3145732
  48.3 3.9 %copy-start.5 = (bf16[512,512]{1,0:T(8,128)(2,1)S(1)}, bf16[512,512]{1,0:T(8,128)(2,1)}, u32[]{:S(2)}) copy-start(bf16[512,512]{1,0:T(8,128)(2,1)} %constant.45.clone.y_odd_ref) | copy-start | bytes 1572868
  48.3 3.8 %copy-start.6 = (bf16[512,512]{1,0:T(8,128)(2,1)S(1)}, bf16[512,512]{1,0:T(8,128)(2,1)}, u32[]{:S(2)}) copy-start(bf16[512,512]{1,0:T(8,128)(2,1)} %constant.44.clone.y_even_ref) | copy-start | bytes 1572868
  48.3 3.8 %copy-start.7 = (bf16[4,256,256]{2,1,0:T(8,128)(2,1)S(1)}, bf16[4,256,256]{2,1,0:T(8,128)(2,1)}, u32[]{:S(2)}) copy-start(bf16[4,256,256]{2,1,0:T(8,128)(2,1)} %constant.43.clone.z_back_ref) | copy-start | bytes 1572868
  48.3 3.8 %copy-start.8 = (bf16[512,512]{1,0:T(8,128)(2,1)S(1)}, bf16[512,512]{1,0:T(8,128)(2,1)}, u32[]{:S(2)}) copy-start(bf16[512,512]{1,0:T(8,128)(2,1)} %constant.42.clone.pick_t_ref) | copy-start | bytes 1572868
  48.3 3.8 %copy-start.9 = (bf16[512,512]{1,0:T(8,128)(2,1)S(1)}, bf16[512,512]{1,0:T(8,128)(2,1)}, u32[]{:S(2)}) copy-start(bf16[512,512]{1,0:T(8,128)(2,1)} %constant.40.clone.fold_t_ref) | copy-start | bytes 1572868
  48.3 3.8 %collective-permute-start = (bf16[16,48,512]{2,1,0:T(8,128)(2,1)S(1)}, bf16[16,48,512]{2,1,0:T(8,128)(2,1)S(1)}, u32[]{:S(2)}, u32[]{:S(2)}) collective-permute-start(bf16[16,48,512]{2,1,0:T(8,128)(2,1)S(1)} %slice.4), channel_id=1, source_target_pairs={{0,16},{16,0},{32,48},{48,32},{64,80},{80,64},{96,112},{112,96},{1... | collective-permute-start | bytes 2359304 | tf_op jit(solution)/shard_map/ppermute | solution.py:374
  58.1 2.0 %collective-permute-start.1 = (bf16[16,4,32,128]{3,2,1,0:T(8,128)(2,1)S(1)}, bf16[16,4,32,128]{3,2,1,0:T(8,128)(2,1)S(1)}, u32[]{:S(2)}, u32[]{:S(2)}) collective-permute-start(bf16[16,4,32,128]{3,2,1,0:T(8,128)(2,1)S(1)} %get-tuple-element.13), channel_id=1, source_target_pairs={{0,16},{16,0},{32,48},{48,32},{64,80},{80,64},{96,112},{112,96},{1... | collective-permute-start | bytes 1572872 | tf_op jit(solution)/shard_map/ppermute | solution.py:377

commit v5 on v4

--- a/solution.py
+++ b/solution.py
@@ -237,9 +237,9 @@
         return rows.reshape(half, -1).astype(f32)
 
     first_row = lax.broadcasted_iota(jnp.int32, (64, half), 0) == 0
+    fulls = [[dot(fold_t_ref[...], spec_s[coil, part].reshape(size, size)) for part in range(2)] for coil in range(2)]
     for coil in range(2):
-        full_re = dot(fold_t_ref[...], spec_s[coil, 0].reshape(size, size))
-        full_im = dot(fold_t_ref[...], spec_s[coil, 1].reshape(size, size))
+        full_re, full_im = fulls[coil]
         for nb in range(2):
             cols = pl.ds(nb * half, half)
             from_re = full_re[:, nb * half : nb * half + half]
@@ -275,12 +275,17 @@
                     even_s[coil, pl.ds(block * 128, 128), at] = back[:, :128]
                     odd_s[coil, pl.ds(block * 128, 128), at] = back[:, 128:]
 
+    wholes = [
+        [
+            [dot(ref[coil, pl.ds(block * half, half), :], table[...]) for ref, table in ((even_s, y_even_ref), (odd_s, y_odd_ref))]
+            for coil in range(2)
+        ]
+        for block in range(2)
+    ]
     for block in range(2):
-        rows = pl.ds(block * half, half)
-        sums = [[jnp.zeros((half, half), f32) for _ in range(2)] for _ in range(2)]
+        sums = [[0.0, 0.0], [0.0, 0.0]]
         for coil in range(2):
-            even = dot(even_s[coil, rows, :], y_even_ref[...])
-            odd = dot(odd_s[coil, rows, :], y_odd_ref[...])
+            even, odd = wholes[block][coil]
             for yb in range(2):
                 full = even + odd if yb == 0 else even - odd
                 re, im = full[:, :half], full[:, half:]

time: 95.1 us -> 94.8 us (level)
  no operation moved by 1% of the time
where the time goes in v5:
time: 94.8 us; the launch traced here: 94.6 us
  blocking collectives  77.9 us (82%)
  Pallas kernels  11.3 us (12%)
  starting transfers between devices  2.33 us (2%)
  waiting for transfers between devices  2.03 us (2%)
    all_to_all x1, blocking collectives, on_device(): lax.all_to_all(packed.reshape(16, 176, 512), 'space', 0, 0, tiled=True)  44.7 us
    all_to_all x1, blocking collectives, on_device(): lax.all_to_all(pair_sum.reshape(64, 32, 128), ('coil', 'space'), 0, 0, ax...  18.4 us
    all_to_all x1, blocking collectives, on_device(): lax.all_to_all(sums, ('space', 'coil'), split_axis=0, concat_axis=0, tile...  14.8 us
    pallas_call x1, Pallas kernels, operator(): pl.pallas_call(operator_kernel, in_specs=[smem] + [vmem] * 11, out_specs=...  5.66 us
    pallas_call x1, Pallas kernels, pack(): pl.pallas_call(pack_kernel, in_specs=[pl.BlockSpec(memory_space=pltpu.SME...  2.82 us
  transfers between devices with their start and end apart: 2, of which 2 were waited for; matrix products, arithmetic and copies ran while one was open for 0% of the time, Pallas kernels for 1%

profile of v5, /device:TPU:1, one launch (start us, length us, event | category | flops | bytes accessed | tf_op | source)
XLA Modules:
  0.0 94.6 jit_solution(7218988688777445130)
XLA Ops:
  0.6 2.8 %pack.1 = bf16[8,2,176,512]{3,2,1,0:T(8,128)(2,1)} custom-call(s32[1]{0:T(128)S(6)} %select_n.7.core_ref, bf16[2,4,8,32,512]{4,3,2,1,0:T(8,128)(2,1)} %sens_ref.1, f32[2,8,32,512]{3,2,1,0:T(8,128)} %dir_ref.3, s32[32,512]{1,0:T(8,128)} %bitcast.14), custom_call_target="tpu_custom_call" | custom-call | tf_op jit(solution)/shard_map/pack/pallas_call | solution.py:101
  3.5 0.0 copy-start
  3.5 0.0 copy-start.1
  3.5 0.0 copy-start.2
  3.5 0.0 copy-start.3
  3.5 0.0 copy-start.4
  3.5 44.7 %all_to_all.21.got_ref = bf16[16,176,512]{2,1,0:T(8,128)(2,1)S(1)} all-to-all(bf16[16,176,512]{2,1,0:T(8,128)(2,1)} %bitcast.12), channel_id=1, replica_groups=mesh['coil'=8,'space'=16] {'space'}, dimensions={0} | all-to-all | bytes 5767168 | tf_op jit(solution)/shard_map/all_to_all | solution.py:378
  48.2 0.1 slice.4
  48.3 0.0 copy-start.5
  48.3 0.0 copy-start.6
  48.3 0.0 copy-start.7
  48.3 0.0 copy-start.8
  48.3 0.0 copy-start.9
  48.3 1.9 %collective-permute-start = (bf16[16,48,512]{2,1,0:T(8,128)(2,1)S(1)}, bf16[16,48,512]{2,1,0:T(8,128)(2,1)S(1)}, u32[]{:S(2)}, u32[]{:S(2)}) collective-permute-start(bf16[16,48,512]{2,1,0:T(8,128)(2,1)S(1)} %slice.4), channel_id=1, source_target_pairs={{0,16},{16,0},{32,48},{48,32},{64,80},{80,64},{96,112},{112,96},{1... | collective-permute-start | bytes 2359304 | tf_op jit(solution)/shard_map/ppermute | solution.py:379
  50.2 0.0 copy-done
  50.2 0.0 copy-done.1
  50.2 0.0 copy-done.2
  50.2 0.0 copy-done.3
  50.2 0.0 copy-done.4
  50.2 1.4 %own_rows.1 = (bf16[2,2,16,16,512]{4,3,2,1,0:T(8,128)(2,1)S(1)}, bf16[16,16,512]{2,1,0:T(8,128)(2,1)S(1)}, f32[3,8,32,128]{3,2,1,0:T(8,128)S(1)}) custom-call(s32[1]{0:T(128)} %bitcast.coil_ref, bf16[16,176,512]{2,1,0:T(8,128)(2,1)S(1)} %all_to_all.21.got_ref, bf16[512,512]{1,0:T(8,128)(2,1)S(1)} %copy-done.2, bf16[512,512]{1,0:T(8,128)(2,1)S(1)} %copy-done.1, ...), custom_call_target="tpu_custom_call" | custom-call | tf_op jit(solution)/shard_map/own_rows/pallas_call | solution.py:192
  51.6 0.5 collective-permute-done.mate_ref
  52.1 0.0 copy-done.5
  52.1 0.0 copy-done.6
  52.1 0.0 copy-done.7
  52.1 5.7 %operator.1 = (f32[16,4,32,128]{3,2,1,0:T(8,128)S(1)}, bf16[16,4,32,128]{3,2,1,0:T(8,128)(2,1)S(1)}) custom-call(s32[1]{0:T(128)} %bitcast.coil_ref, bf16[16,176,512]{2,1,0:T(8,128)(2,1)S(1)} %all_to_all.21.got_ref, bf16[16,48,512]{2,1,0:T(8,128)(2,1)S(1)} %collective-permute-done.mate_ref, bf16[2,2,16,16,512]{4,3,2,1,0:T(8,128)(2,1)S(1)} %get-tuple-element.10.ready_ref, ...), custom_call_target="tpu_custom_call" | custom-call | tf_op jit(solution)/shard_map/operator/pallas_call | solution.py:307
  57.8 0.5 collective-permute-start.1
  58.3 1.5 %collective-permute-done.1 = bf16[16,4,32,128]{3,2,1,0:T(8,128)(2,1)S(1)} collective-permute-done((bf16[16,4,32,128]{3,2,1,0:T(8,128)(2,1)S(1)}, bf16[16,4,32,128]{3,2,1,0:T(8,128)(2,1)S(1)}, u32[]{:S(2)}, u32[]{:S(2)}) %collective-permute-start.1) | collective-permute-done | bytes 524320 | tf_op jit(solution)/shard_map/ppermute | solution.py:382
  59.8 0.2 add_convert_fusion
  60.0 18.4 %all_to_all.22 = bf16[64,32,128]{2,1,0:T(8,128)(2,1)S(1)} all-to-all(bf16[64,32,128]{2,1,0:T(8,128)(2,1)S(1)} %bitcast.13), channel_id=1, replica_groups={{0,32,64,96,1,33,65,97,2,34,66,98,3,35,67,99,4,36,68,100,5,37,69,101,6,..., dimensions={0} | all-to-all | bytes 1048576 | tf_op jit(solution)/shard_map/all_to_all | solution.py:383
  78.4 0.3 sums.1
  78.7 14.8 %all_to_all.23 = f32[128,1,128]{2,1,0:T(1,128)S(1)} all-to-all(f32[128,1,128]{2,1,0:T(1,128)S(1)} %bitcast.11), channel_id=1, replica_groups=mesh['coil'=8,'space'=16] {'space','coil'}, dimensions={0} | all-to-all | bytes 131072 | tf_op jit(solution)/shard_map/all_to_all | solution.py:399
  93.5 1.1 %final.1 = (f32[2,8,32,64]{3,2,1,0:T(8,128)}, f32[2,8,32,64]{3,2,1,0:T(8,128)}, f32[2,8,32,64]{3,2,1,0:T(8,128)}) custom-call(f32[128,128]{1,0:T(8,128)S(1)} %bitcast.10, f32[8,32,128]{2,1,0:T(8,128)S(1)} %get-tuple-element.16.applied_ref, f32[3,8,32,128]{3,2,1,0:T(8,128)S(1)} %get-tuple-element.14.own_ref), custom_call_target="tpu_custom_call" | custom-call | tf_op jit(solution)/shard_map/final/pallas_call | solution.py:400
  (2 shorter events, 0.0 us)
Async XLA Ops:
  3.5 46.7 %copy-start = (f32[2,8,32,512]{3,2,1,0:T(8,128)S(1)}, f32[2,8,32,512]{3,2,1,0:T(8,128)}, u32[]{:S(2)}) copy-start(f32[2,8,32,512]{3,2,1,0:T(8,128)} %dir_ref.3) | copy-start | bytes 3145732
  3.5 46.7 %copy-start.1 = (bf16[512,512]{1,0:T(8,128)(2,1)S(1)}, bf16[512,512]{1,0:T(8,128)(2,1)}, u32[]{:S(2)}) copy-start(bf16[512,512]{1,0:T(8,128)(2,1)} %constant.41.clone.pick_ref) | copy-start | bytes 1572868
  3.5 46.7 %copy-start.2 = (bf16[512,512]{1,0:T(8,128)(2,1)S(1)}, bf16[512,512]{1,0:T(8,128)(2,1)}, u32[]{:S(2)}) copy-start(bf16[512,512]{1,0:T(8,128)(2,1)} %constant.39.clone.fold_ref) | copy-start | bytes 1572868
  3.5 46.7 %copy-start.3 = (f32[2,8,32,512]{3,2,1,0:T(8,128)S(1)}, f32[2,8,32,512]{3,2,1,0:T(8,128)}, u32[]{:S(2)}) copy-start(f32[2,8,32,512]{3,2,1,0:T(8,128)} %res_ref.1) | copy-start | bytes 3145732
  3.5 46.7 %copy-start.4 = (f32[2,8,32,512]{3,2,1,0:T(8,128)S(1)}, f32[2,8,32,512]{3,2,1,0:T(8,128)}, u32[]{:S(2)}) copy-start(f32[2,8,32,512]{3,2,1,0:T(8,128)} %img_ref.1) | copy-start | bytes 3145732
  48.3 3.9 %copy-start.5 = (bf16[512,512]{1,0:T(8,128)(2,1)S(1)}, bf16[512,512]{1,0:T(8,128)(2,1)}, u32[]{:S(2)}) copy-start(bf16[512,512]{1,0:T(8,128)(2,1)} %constant.45.clone.y_odd_ref) | copy-start | bytes 1572868
  48.3 3.8 %copy-start.6 = (bf16[512,512]{1,0:T(8,128)(2,1)S(1)}, bf16[512,512]{1,0:T(8,128)(2,1)}, u32[]{:S(2)}) copy-start(bf16[512,512]{1,0:T(8,128)(2,1)} %constant.44.clone.y_even_ref) | copy-start | bytes 1572868
  48.3 3.8 %copy-start.7 = (bf16[4,256,256]{2,1,0:T(8,128)(2,1)S(1)}, bf16[4,256,256]{2,1,0:T(8,128)(2,1)}, u32[]{:S(2)}) copy-start(bf16[4,256,256]{2,1,0:T(8,128)(2,1)} %constant.43.clone.z_back_ref) | copy-start | bytes 1572868
  48.3 3.8 %copy-start.8 = (bf16[512,512]{1,0:T(8,128)(2,1)S(1)}, bf16[512,512]{1,0:T(8,128)(2,1)}, u32[]{:S(2)}) copy-start(bf16[512,512]{1,0:T(8,128)(2,1)} %constant.42.clone.pick_t_ref) | copy-start | bytes 1572868
  48.3 3.8 %copy-start.9 = (bf16[512,512]{1,0:T(8,128)(2,1)S(1)}, bf16[512,512]{1,0:T(8,128)(2,1)}, u32[]{:S(2)}) copy-start(bf16[512,512]{1,0:T(8,128)(2,1)} %constant.40.clone.fold_t_ref) | copy-start | bytes 1572868
  48.3 3.8 %collective-permute-start = (bf16[16,48,512]{2,1,0:T(8,128)(2,1)S(1)}, bf16[16,48,512]{2,1,0:T(8,128)(2,1)S(1)}, u32[]{:S(2)}, u32[]{:S(2)}) collective-permute-start(bf16[16,48,512]{2,1,0:T(8,128)(2,1)S(1)} %slice.4), channel_id=1, source_target_pairs={{0,16},{16,0},{32,48},{48,32},{64,80},{80,64},{96,112},{112,96},{1... | collective-permute-start | bytes 2359304 | tf_op jit(solution)/shard_map/ppermute | solution.py:379
  57.8 2.0 %collective-permute-start.1 = (bf16[16,4,32,128]{3,2,1,0:T(8,128)(2,1)S(1)}, bf16[16,4,32,128]{3,2,1,0:T(8,128)(2,1)S(1)}, u32[]{:S(2)}, u32[]{:S(2)}) collective-permute-start(bf16[16,4,32,128]{3,2,1,0:T(8,128)(2,1)S(1)} %get-tuple-element.13), channel_id=1, source_target_pairs={{0,16},{16,0},{32,48},{48,32},{64,80},{80,64},{96,112},{112,96},{1... | collective-permute-start | bytes 1572872 | tf_op jit(solution)/shard_map/ppermute | solution.py:382

commit v6 on v5

--- a/solution.py
+++ b/solution.py
@@ -39,7 +39,8 @@
         return np.block([[cos_g, -sin_g], [sin_g, cos_g]])
 
     quarter = half // 4
-    outs = [fold, fold.T, pick, pick.T]
+    by_core = fold.T.reshape(length, 16, 2, 16).transpose(2, 0, 1, 3).reshape(2, length, half)
+    outs = [fold, by_core, pick, pick.T]
     outs.append(
         np.stack(
             [
@@ -152,7 +153,9 @@
 
 
 def own_rows_kernel(
-    coil_ref, got_ref, fold_ref, pick_ref, dir_ref, res_ref, img_ref, out_ref, mask_ref, own_ref, image_s, own_s, sems
+    coil_ref, got_ref, fold_ref, fold_t_ref, pick_ref, dir_ref, res_ref, img_ref,
+    share_ref, mask_ref, own_ref,
+    image_s, spec_s, own_s, sems,
 ):
     core = coil_ref[0] % 2
     own_lanes = pl.ds(pl.multiple_of(coil_ref[0] // 2 * 128, 128), 128)
@@ -164,11 +167,14 @@
         copy.start()
 
     def store(coil, part, start, value):
-        out_ref[coil, part, :, :, pl.ds(start, 128)] = value.reshape(16, 16, 128)
+        spec_s[coil, part, :, pl.ds(start, 128)] = value
 
     dir_parts = [got_ref.at[:, pl.ds(128 + part * 16, 16), :] for part in range(2)]
     spectrum_rows(got_ref, dir_parts, core, fold_ref, image_s, store)
     mask_ref[...] = mask_columns(got_ref[:, pl.ds(160, 16), :], pick_ref)
+    for coil in range(2):
+        for part in range(2):
+            share_ref[coil, part] = dot(fold_t_ref[core], spec_s[coil, part])
     for copy in own_copies:
         copy.wait()
     for index in range(3):
@@ -186,30 +192,31 @@
     return jnp.where(lower, re, moved), jnp.where(lower, moved, im)
 
 
-def own_rows(coil, got, fold, pick, direction, residual, image):
+def own_rows(coil, got, fold, fold_t, pick, direction, residual, image):
     hbm = pl.BlockSpec(memory_space=pltpu.HBM)
     vmem = pl.BlockSpec(memory_space=pltpu.VMEM)
     return pl.pallas_call(
         own_rows_kernel,
-        in_specs=[pl.BlockSpec(memory_space=pltpu.SMEM)] + [vmem] * 3 + [hbm] * 3,
+        in_specs=[pl.BlockSpec(memory_space=pltpu.SMEM)] + [vmem] * 4 + [hbm] * 3,
         out_specs=[vmem] * 3,
         out_shape=[
-            jax.ShapeDtypeStruct((2, 2, 16, 16, 512), jnp.bfloat16),
+            jax.ShapeDtypeStruct((2, 2, 512, 512), jnp.float32),
             jax.ShapeDtypeStruct((16, 16, 512), jnp.bfloat16),
             jax.ShapeDtypeStruct((3, 8, 32, 128), jnp.float32),
         ],
         scratch_shapes=[
+            pltpu.VMEM((2, 2, 256, 512), jnp.bfloat16),
             pltpu.VMEM((2, 2, 256, 512), jnp.bfloat16),
             pltpu.VMEM((3, 2, 8, 32, 128), jnp.float32),
             pltpu.SemaphoreType.DMA((3,)),
         ],
         compiler_params=pltpu.CompilerParams(vmem_limit_bytes=16 * 1024 * 1024),
         name="own_rows",
-    )(coil, got, fold, pick, direction, residual, image)
+    )(coil, got, fold, fold_t, pick, direction, residual, image)
 
 
 def operator_kernel(
-    coil_ref, got_ref, mate_ref, ready_ref, mask_ref, fold_ref, fold_t_ref, pick_ref, pick_t_ref,
+    coil_ref, got_ref, mate_ref, share_ref, mask_ref, fold_ref, fold_t_ref, pick_ref, pick_t_ref,
     z_back_ref, y_even_ref, y_odd_ref,
     keep_ref, send_ref,
     image_s, spec_s, even_s, odd_s, mask_t_s, mask_s,
@@ -220,13 +227,10 @@
     bf16 = jnp.bfloat16
     core = coil_ref[0] % 2
     def store(coil, part, start, value):
-        spec_s[coil, part, :, 1 - core, :, pl.ds(start, 128)] = value.reshape(16, 16, 128)
+        spec_s[coil, part, :, pl.ds(start, 128)] = value
 
     dir_parts = [mate_ref.at[:, pl.ds(part * 16, 16), :] for part in range(2)]
     spectrum_rows(got_ref, dir_parts, 1 - core, fold_ref, image_s, store)
-    for coil in range(2):
-        for part in range(2):
-            spec_s[coil, part, :, core] = ready_ref[coil, part]
 
     mask_t_s[:, core] = mask_ref[...]
     mask_t_s[:, 1 - core] = mask_columns(mate_ref[:, pl.ds(32, 16), :], pick_ref)
@@ -237,7 +241,9 @@
         return rows.reshape(half, -1).astype(f32)
 
     first_row = lax.broadcasted_iota(jnp.int32, (64, half), 0) == 0
-    fulls = [[dot(fold_t_ref[...], spec_s[coil, part].reshape(size, size)) for part in range(2)] for coil in range(2)]
+    fulls = [
+        [share_ref[coil, part] + dot(fold_t_ref[1 - core], spec_s[coil, part]) for part in range(2)] for coil in range(2)
+    ]
     for coil in range(2):
         full_re, full_im = fulls[coil]
         for nb in range(2):
@@ -301,7 +307,7 @@
                 send_ref[slabs, yb * 2 + lb] = jnp.where(core == 0, odd, even).reshape(8, 32, 128).astype(bf16)
 
 
-def operator(coil, got, mate, ready, mask, fold_tabs):
+def operator(coil, got, mate, share, mask, fold_tabs):
     smem = pl.BlockSpec(memory_space=pltpu.SMEM)
     vmem = pl.BlockSpec(memory_space=pltpu.VMEM)
     return pl.pallas_call(
@@ -314,7 +320,7 @@
         ],
         scratch_shapes=[
             pltpu.VMEM((2, 2, 256, 512), jnp.bfloat16),
-            pltpu.VMEM((2, 2, 16, 2, 16, 512), jnp.bfloat16),
+            pltpu.VMEM((2, 2, 256, 512), jnp.bfloat16),
             pltpu.VMEM((2, 512, 512), jnp.bfloat16),
             pltpu.VMEM((2, 512, 512), jnp.bfloat16),
             pltpu.VMEM((16, 2, 16, 512), jnp.bfloat16),
@@ -322,7 +328,7 @@
         ],
         compiler_params=pltpu.CompilerParams(vmem_limit_bytes=32 * 1024 * 1024),
         name="operator",
-    )(coil, got, mate, ready, mask, *fold_tabs)
+    )(coil, got, mate, share, mask, *fold_tabs)
 
 
 def sums_kernel(part_ref, own_ref, applied_ref, sums_ref):
@@ -377,8 +383,8 @@
     packed = pack(coil % 2, sensitivity, direction, sampling.T)
     got = lax.all_to_all(packed.reshape(16, 176, 512), "space", 0, 0, tiled=True)
     mate = lax.ppermute(got[:, 128:], "coil", mates)
-    ready, mask, own = own_rows(coil, got, fold_tabs[0], fold_tabs[2], direction, residual, image)
-    keep, send = operator(coil, got, mate, ready, mask, fold_tabs)
+    share, mask, own = own_rows(coil, got, *fold_tabs[:3], direction, residual, image)
+    keep, send = operator(coil, got, mate, share, mask, fold_tabs)
     pair_sum = (keep + lax.ppermute(send, "coil", mates)).astype(jnp.bfloat16)
     parts = lax.all_to_all(
         pair_sum.reshape(64, 32, 128), ("coil", "space"), 0, 0, axis_index_groups=same_core, tiled=True

time: 94.8 us -> 94.7 us (level)
  transfers between devices with their start and end apart: 2 -> 2, of which waited for: 2 -> 1; matrix products, arithmetic and copies ran while one was open for 0% -> 0% of each run, Pallas kernels for 1% -> 2%
where the time goes in v6:
time: 94.7 us; the launch traced here: 94.4 us
  blocking collectives  77.9 us (82%)
  Pallas kernels  11.6 us (12%)
  starting transfers between devices  2.22 us (2%)
  waiting for transfers between devices  1.65 us (2%)
    all_to_all x1, blocking collectives, on_device(): lax.all_to_all(packed.reshape(16, 176, 512), 'space', 0, 0, tiled=True)  44.7 us
    all_to_all x1, blocking collectives, on_device(): lax.all_to_all(pair_sum.reshape(64, 32, 128), ('coil', 'space'), 0, 0, ax...  18.5 us
    all_to_all x1, blocking collectives, on_device(): lax.all_to_all(sums, ('space', 'coil'), split_axis=0, concat_axis=0, tile...  14.7 us
    pallas_call x1, Pallas kernels, operator(): pl.pallas_call(operator_kernel, in_specs=[smem] + [vmem] * 11, out_specs=...  5.42 us
    pallas_call x1, Pallas kernels, pack(): pl.pallas_call(pack_kernel, in_specs=[pl.BlockSpec(memory_space=pltpu.SME...  2.82 us
    pallas_call x1, Pallas kernels, own_rows(): pl.pallas_call(own_rows_kernel, in_specs=[pl.BlockSpec(memory_space=pltpu...  1.95 us
  transfers between devices with their start and end apart: 2, of which 1 were waited for; matrix products, arithmetic and copies ran while one was open for 0% of the time, Pallas kernels for 2%

profile of v6, /device:TPU:1, one launch (start us, length us, event | category | flops | bytes accessed | tf_op | source)
XLA Modules:
  0.0 94.4 jit_solution(15157859328891449854)
XLA Ops:
  0.6 2.8 %pack.1 = bf16[8,2,176,512]{3,2,1,0:T(8,128)(2,1)} custom-call(s32[1]{0:T(128)S(6)} %select_n.7.core_ref, bf16[2,4,8,32,512]{4,3,2,1,0:T(8,128)(2,1)} %sens_ref.1, f32[2,8,32,512]{3,2,1,0:T(8,128)} %dir_ref.3, s32[32,512]{1,0:T(8,128)} %bitcast.14), custom_call_target="tpu_custom_call" | custom-call | tf_op jit(solution)/shard_map/pack/pallas_call | solution.py:102
  3.5 0.0 copy-start
  3.5 0.0 copy-start.1
  3.5 0.0 copy-start.2
  3.5 0.0 copy-start.3
  3.5 0.0 copy-start.4
  3.5 0.0 copy-start.5
  3.5 44.7 %all_to_all.21.got_ref = bf16[16,176,512]{2,1,0:T(8,128)(2,1)S(1)} all-to-all(bf16[16,176,512]{2,1,0:T(8,128)(2,1)} %bitcast.12), channel_id=1, replica_groups=mesh['coil'=8,'space'=16] {'space'}, dimensions={0} | all-to-all | bytes 5767168 | tf_op jit(solution)/shard_map/all_to_all | solution.py:384
  48.2 0.1 slice.4
  48.3 0.0 copy-start.6
  48.3 0.0 copy-start.7
  48.3 0.0 copy-start.8
  48.3 0.0 copy-start.9
  48.3 1.9 %collective-permute-start = (bf16[16,48,512]{2,1,0:T(8,128)(2,1)S(1)}, bf16[16,48,512]{2,1,0:T(8,128)(2,1)S(1)}, u32[]{:S(2)}, u32[]{:S(2)}) collective-permute-start(bf16[16,48,512]{2,1,0:T(8,128)(2,1)S(1)} %slice.4), channel_id=1, source_target_pairs={{0,16},{16,0},{32,48},{48,32},{64,80},{80,64},{96,112},{112,96},{1... | collective-permute-start | bytes 2359304 | tf_op jit(solution)/shard_map/ppermute | solution.py:385
  50.2 0.0 copy-done
  50.2 0.0 copy-done.1
  50.2 0.0 copy-done.2
  50.2 0.0 copy-done.3
  50.2 0.0 copy-done.4
  50.2 0.0 copy-done.5
  50.2 1.9 %own_rows.1 = (f32[2,2,512,512]{3,2,1,0:T(8,128)S(1)}, bf16[16,16,512]{2,1,0:T(8,128)(2,1)S(1)}, f32[3,8,32,128]{3,2,1,0:T(8,128)S(1)}) custom-call(s32[1]{0:T(128)} %bitcast.coil_ref, bf16[16,176,512]{2,1,0:T(8,128)(2,1)S(1)} %all_to_all.21.got_ref, bf16[512,512]{1,0:T(8,128)(2,1)S(1)} %copy-done.3, bf16[2,512,256]{2,1,0:T(8,128)(2,1)S(1)} %copy-done.2, ...), custom_call_target="tpu_custom_call" | custom-call | tf_op jit(solution)/shard_map/own_rows/pallas_call | solution.py:198
  52.2 0.0 collective-permute-done.mate_ref
  52.2 0.0 copy-done.6
  52.2 0.0 copy-done.7
  52.2 5.4 %operator.1 = (f32[16,4,32,128]{3,2,1,0:T(8,128)S(1)}, bf16[16,4,32,128]{3,2,1,0:T(8,128)(2,1)S(1)}) custom-call(s32[1]{0:T(128)} %bitcast.coil_ref, bf16[16,176,512]{2,1,0:T(8,128)(2,1)S(1)} %all_to_all.21.got_ref, bf16[16,48,512]{2,1,0:T(8,128)(2,1)S(1)} %collective-permute-done.mate_ref, f32[2,2,512,512]{3,2,1,0:T(8,128)S(1)} %get-tuple-element.10.share_ref, ...), custom_call_target="tpu_custom_call" | custom-call | tf_op jit(solution)/shard_map/operator/pallas_call | solution.py:313
  57.7 0.3 collective-permute-start.1
  58.0 1.6 %collective-permute-done.1 = bf16[16,4,32,128]{3,2,1,0:T(8,128)(2,1)S(1)} collective-permute-done((bf16[16,4,32,128]{3,2,1,0:T(8,128)(2,1)S(1)}, bf16[16,4,32,128]{3,2,1,0:T(8,128)(2,1)S(1)}, u32[]{:S(2)}, u32[]{:S(2)}) %collective-permute-start.1) | collective-permute-done | bytes 524320 | tf_op jit(solution)/shard_map/ppermute | solution.py:388
  59.7 0.2 add_convert_fusion
  59.8 18.5 %all_to_all.22 = bf16[64,32,128]{2,1,0:T(8,128)(2,1)S(1)} all-to-all(bf16[64,32,128]{2,1,0:T(8,128)(2,1)S(1)} %bitcast.13), channel_id=1, replica_groups={{0,32,64,96,1,33,65,97,2,34,66,98,3,35,67,99,4,36,68,100,5,37,69,101,6,..., dimensions={0} | all-to-all | bytes 1048576 | tf_op jit(solution)/shard_map/all_to_all | solution.py:389
  78.4 0.3 sums.1
  78.7 14.7 %all_to_all.23 = f32[128,1,128]{2,1,0:T(1,128)S(1)} all-to-all(f32[128,1,128]{2,1,0:T(1,128)S(1)} %bitcast.11), channel_id=1, replica_groups=mesh['coil'=8,'space'=16] {'space','coil'}, dimensions={0} | all-to-all | bytes 131072 | tf_op jit(solution)/shard_map/all_to_all | solution.py:405
  93.3 1.1 %final.1 = (f32[2,8,32,64]{3,2,1,0:T(8,128)}, f32[2,8,32,64]{3,2,1,0:T(8,128)}, f32[2,8,32,64]{3,2,1,0:T(8,128)}) custom-call(f32[128,128]{1,0:T(8,128)S(1)} %bitcast.10, f32[8,32,128]{2,1,0:T(8,128)S(1)} %get-tuple-element.16.applied_ref, f32[3,8,32,128]{3,2,1,0:T(8,128)S(1)} %get-tuple-element.14.own_ref), custom_call_target="tpu_custom_call" | custom-call | tf_op jit(solution)/shard_map/final/pallas_call | solution.py:406
  (2 shorter events, 0.0 us)
Async XLA Ops:
  3.5 46.7 %copy-start = (f32[2,8,32,512]{3,2,1,0:T(8,128)S(1)}, f32[2,8,32,512]{3,2,1,0:T(8,128)}, u32[]{:S(2)}) copy-start(f32[2,8,32,512]{3,2,1,0:T(8,128)} %dir_ref.3) | copy-start | bytes 3145732
  3.5 46.7 %copy-start.1 = (bf16[512,512]{1,0:T(8,128)(2,1)S(1)}, bf16[512,512]{1,0:T(8,128)(2,1)}, u32[]{:S(2)}) copy-start(bf16[512,512]{1,0:T(8,128)(2,1)} %constant.41.clone.pick_ref) | copy-start | bytes 1572868
  3.5 46.7 %copy-start.2 = (bf16[2,512,256]{2,1,0:T(8,128)(2,1)S(1)}, bf16[2,512,256]{2,1,0:T(8,128)(2,1)}, u32[]{:S(2)}) copy-start(bf16[2,512,256]{2,1,0:T(8,128)(2,1)} %constant.40.clone.fold_t_ref) | copy-start | bytes 1572868
  3.5 46.7 %copy-start.3 = (bf16[512,512]{1,0:T(8,128)(2,1)S(1)}, bf16[512,512]{1,0:T(8,128)(2,1)}, u32[]{:S(2)}) copy-start(bf16[512,512]{1,0:T(8,128)(2,1)} %constant.39.clone.fold_ref) | copy-start | bytes 1572868
  3.5 46.7 %copy-start.4 = (f32[2,8,32,512]{3,2,1,0:T(8,128)S(1)}, f32[2,8,32,512]{3,2,1,0:T(8,128)}, u32[]{:S(2)}) copy-start(f32[2,8,32,512]{3,2,1,0:T(8,128)} %res_ref.1) | copy-start | bytes 3145732
  3.5 46.7 %copy-start.5 = (f32[2,8,32,512]{3,2,1,0:T(8,128)S(1)}, f32[2,8,32,512]{3,2,1,0:T(8,128)}, u32[]{:S(2)}) copy-start(f32[2,8,32,512]{3,2,1,0:T(8,128)} %img_ref.1) | copy-start | bytes 3145732
  48.3 3.9 %copy-start.6 = (bf16[512,512]{1,0:T(8,128)(2,1)S(1)}, bf16[512,512]{1,0:T(8,128)(2,1)}, u32[]{:S(2)}) copy-start(bf16[512,512]{1,0:T(8,128)(2,1)} %constant.45.clone.y_odd_ref) | copy-start | bytes 1572868
  48.3 3.9 %copy-start.7 = (bf16[512,512]{1,0:T(8,128)(2,1)S(1)}, bf16[512,512]{1,0:T(8,128)(2,1)}, u32[]{:S(2)}) copy-start(bf16[512,512]{1,0:T(8,128)(2,1)} %constant.44.clone.y_even_ref) | copy-start | bytes 1572868
  48.3 3.9 %copy-start.8 = (bf16[4,256,256]{2,1,0:T(8,128)(2,1)S(1)}, bf16[4,256,256]{2,1,0:T(8,128)(2,1)}, u32[]{:S(2)}) copy-start(bf16[4,256,256]{2,1,0:T(8,128)(2,1)} %constant.43.clone.z_back_ref) | copy-start | bytes 1572868
  48.3 3.9 %copy-start.9 = (bf16[512,512]{1,0:T(8,128)(2,1)S(1)}, bf16[512,512]{1,0:T(8,128)(2,1)}, u32[]{:S(2)}) copy-start(bf16[512,512]{1,0:T(8,128)(2,1)} %constant.42.clone.pick_t_ref) | copy-start | bytes 1572868
  48.3 3.9 %collective-permute-start = (bf16[16,48,512]{2,1,0:T(8,128)(2,1)S(1)}, bf16[16,48,512]{2,1,0:T(8,128)(2,1)S(1)}, u32[]{:S(2)}, u32[]{:S(2)}) collective-permute-start(bf16[16,48,512]{2,1,0:T(8,128)(2,1)S(1)} %slice.4), channel_id=1, source_target_pairs={{0,16},{16,0},{32,48},{48,32},{64,80},{80,64},{96,112},{112,96},{1... | collective-permute-start | bytes 2359304 | tf_op jit(solution)/shard_map/ppermute | solution.py:385
  57.7 2.0 %collective-permute-start.1 = (bf16[16,4,32,128]{3,2,1,0:T(8,128)(2,1)S(1)}, bf16[16,4,32,128]{3,2,1,0:T(8,128)(2,1)S(1)}, u32[]{:S(2)}, u32[]{:S(2)}) collective-permute-start(bf16[16,4,32,128]{3,2,1,0:T(8,128)(2,1)S(1)} %get-tuple-element.13), channel_id=1, source_target_pairs={{0,16},{16,0},{32,48},{48,32},{64,80},{80,64},{96,112},{112,96},{1... | collective-permute-start | bytes 1572872 | tf_op jit(solution)/shard_map/ppermute | solution.py:388

commit v7 on v6

--- a/solution.py
+++ b/solution.py
@@ -226,30 +226,30 @@
     f32 = jnp.float32
     bf16 = jnp.bfloat16
     core = coil_ref[0] % 2
-    def store(coil, part, start, value):
-        spec_s[coil, part, :, pl.ds(start, 128)] = value
-
-    dir_parts = [mate_ref.at[:, pl.ds(part * 16, 16), :] for part in range(2)]
-    spectrum_rows(got_ref, dir_parts, 1 - core, fold_ref, image_s, store)
-
     mask_t_s[:, core] = mask_ref[...]
     mask_t_s[:, 1 - core] = mask_columns(mate_ref[:, pl.ds(32, 16), :], pick_ref)
     mask_s[...] = dot(pick_t_ref[...], mask_t_s[...].reshape(size, size)).T
 
+    def store(coil, part, start, value):
+        spec_s[coil, part, :, pl.ds(start, 128)] = value
+
+    dir_parts = [mate_ref.at[:, pl.ds(part * 16, 16), :] for part in range(2)]
+    spectrum_rows(got_ref, dir_parts, 1 - core, fold_ref, image_s, store)
+
     def sens(coil, part, block, lanes):
         rows = got_ref[pl.ds(block * 8, 8), pl.ds((part * 2 + coil) * 32, 32), lanes]
         return rows.reshape(half, -1).astype(f32)
 
     first_row = lax.broadcasted_iota(jnp.int32, (64, half), 0) == 0
     fulls = [
-        [share_ref[coil, part] + dot(fold_t_ref[1 - core], spec_s[coil, part]) for part in range(2)] for coil in range(2)
+        [dot(fold_t_ref[1 - core], spec_s[coil, part]) for part in range(2)] for coil in range(2)
     ]
     for coil in range(2):
         full_re, full_im = fulls[coil]
         for nb in range(2):
             cols = pl.ds(nb * half, half)
-            from_re = full_re[:, nb * half : nb * half + half]
-            from_im = full_im[:, nb * half : nb * half + half]
+            from_re = full_re[:, nb * half : nb * half + half] + share_ref[coil, 0, :, cols]
+            from_im = full_im[:, nb * half : nb * half + half] + share_ref[coil, 1, :, cols]
 
             def kept(rest):
                 pieces = [[], []]

time: 94.7 us -> 94.7 us (level)
  no operation moved by 1% of the time
where the time goes in v7:
time: 94.7 us; the launch traced here: 94.4 us
  blocking collectives  77.9 us (82%)
  Pallas kernels  11.6 us (12%)
  starting transfers between devices  2.22 us (2%)
  waiting for transfers between devices  1.64 us (2%)
    all_to_all x1, blocking collectives, on_device(): lax.all_to_all(packed.reshape(16, 176, 512), 'space', 0, 0, tiled=True)  44.7 us
    all_to_all x1, blocking collectives, on_device(): lax.all_to_all(pair_sum.reshape(64, 32, 128), ('coil', 'space'), 0, 0, ax...  18.5 us
    all_to_all x1, blocking collectives, on_device(): lax.all_to_all(sums, ('space', 'coil'), split_axis=0, concat_axis=0, tile...  14.7 us
    pallas_call x1, Pallas kernels, operator(): pl.pallas_call(operator_kernel, in_specs=[smem] + [vmem] * 11, out_specs=...  5.43 us
    pallas_call x1, Pallas kernels, pack(): pl.pallas_call(pack_kernel, in_specs=[pl.BlockSpec(memory_space=pltpu.SME...  2.82 us
    pallas_call x1, Pallas kernels, own_rows(): pl.pallas_call(own_rows_kernel, in_specs=[pl.BlockSpec(memory_space=pltpu...  1.95 us
  transfers between devices with their start and end apart: 2, of which 1 were waited for; matrix products, arithmetic and copies ran while one was open for 0% of the time, Pallas kernels for 2%

profile of v7, /device:TPU:1, one launch (start us, length us, event | category | flops | bytes accessed | tf_op | source)
XLA Modules:
  0.0 94.4 jit_solution(3962645532028212347)
XLA Ops:
  0.6 2.8 %pack.1 = bf16[8,2,176,512]{3,2,1,0:T(8,128)(2,1)} custom-call(s32[1]{0:T(128)S(6)} %select_n.7.core_ref, bf16[2,4,8,32,512]{4,3,2,1,0:T(8,128)(2,1)} %sens_ref.1, f32[2,8,32,512]{3,2,1,0:T(8,128)} %dir_ref.3, s32[32,512]{1,0:T(8,128)} %bitcast.14), custom_call_target="tpu_custom_call" | custom-call | tf_op jit(solution)/shard_map/pack/pallas_call | solution.py:102
  3.5 0.0 copy-start
  3.5 0.0 copy-start.1
  3.5 0.0 copy-start.2
  3.5 0.0 copy-start.3
  3.5 0.0 copy-start.4
  3.5 0.0 copy-start.5
  3.5 44.7 %all_to_all.21.got_ref = bf16[16,176,512]{2,1,0:T(8,128)(2,1)S(1)} all-to-all(bf16[16,176,512]{2,1,0:T(8,128)(2,1)} %bitcast.12), channel_id=1, replica_groups=mesh['coil'=8,'space'=16] {'space'}, dimensions={0} | all-to-all | bytes 5767168 | tf_op jit(solution)/shard_map/all_to_all | solution.py:384
  48.2 0.1 slice.4
  48.3 0.0 copy-start.6
  48.3 0.0 copy-start.7
  48.3 0.0 copy-start.8
  48.3 0.0 copy-start.9
  48.3 1.9 %collective-permute-start = (bf16[16,48,512]{2,1,0:T(8,128)(2,1)S(1)}, bf16[16,48,512]{2,1,0:T(8,128)(2,1)S(1)}, u32[]{:S(2)}, u32[]{:S(2)}) collective-permute-start(bf16[16,48,512]{2,1,0:T(8,128)(2,1)S(1)} %slice.4), channel_id=1, source_target_pairs={{0,16},{16,0},{32,48},{48,32},{64,80},{80,64},{96,112},{112,96},{1... | collective-permute-start | bytes 2359304 | tf_op jit(solution)/shard_map/ppermute | solution.py:385
  50.2 0.0 copy-done
  50.2 0.0 copy-done.1
  50.2 0.0 copy-done.2
  50.2 0.0 copy-done.3
  50.2 0.0 copy-done.4
  50.2 0.0 copy-done.5
  50.2 1.9 %own_rows.1 = (f32[2,2,512,512]{3,2,1,0:T(8,128)S(1)}, bf16[16,16,512]{2,1,0:T(8,128)(2,1)S(1)}, f32[3,8,32,128]{3,2,1,0:T(8,128)S(1)}) custom-call(s32[1]{0:T(128)} %bitcast.coil_ref, bf16[16,176,512]{2,1,0:T(8,128)(2,1)S(1)} %all_to_all.21.got_ref, bf16[512,512]{1,0:T(8,128)(2,1)S(1)} %copy-done.3, bf16[2,512,256]{2,1,0:T(8,128)(2,1)S(1)} %copy-done.2, ...), custom_call_target="tpu_custom_call" | custom-call | tf_op jit(solution)/shard_map/own_rows/pallas_call | solution.py:198
  52.2 0.0 collective-permute-done.mate_ref
  52.2 0.0 copy-done.6
  52.2 0.0 copy-done.7
  52.2 5.4 %operator.1 = (f32[16,4,32,128]{3,2,1,0:T(8,128)S(1)}, bf16[16,4,32,128]{3,2,1,0:T(8,128)(2,1)S(1)}) custom-call(s32[1]{0:T(128)} %bitcast.coil_ref, bf16[16,176,512]{2,1,0:T(8,128)(2,1)S(1)} %all_to_all.21.got_ref, bf16[16,48,512]{2,1,0:T(8,128)(2,1)S(1)} %collective-permute-done.mate_ref, f32[2,2,512,512]{3,2,1,0:T(8,128)S(1)} %get-tuple-element.10.share_ref, ...), custom_call_target="tpu_custom_call" | custom-call | tf_op jit(solution)/shard_map/operator/pallas_call | solution.py:313
  57.7 0.3 collective-permute-start.1
  58.0 1.6 %collective-permute-done.1 = bf16[16,4,32,128]{3,2,1,0:T(8,128)(2,1)S(1)} collective-permute-done((bf16[16,4,32,128]{3,2,1,0:T(8,128)(2,1)S(1)}, bf16[16,4,32,128]{3,2,1,0:T(8,128)(2,1)S(1)}, u32[]{:S(2)}, u32[]{:S(2)}) %collective-permute-start.1) | collective-permute-done | bytes 524320 | tf_op jit(solution)/shard_map/ppermute | solution.py:388
  59.7 0.2 add_convert_fusion
  59.8 18.5 %all_to_all.22 = bf16[64,32,128]{2,1,0:T(8,128)(2,1)S(1)} all-to-all(bf16[64,32,128]{2,1,0:T(8,128)(2,1)S(1)} %bitcast.13), channel_id=1, replica_groups={{0,32,64,96,1,33,65,97,2,34,66,98,3,35,67,99,4,36,68,100,5,37,69,101,6,..., dimensions={0} | all-to-all | bytes 1048576 | tf_op jit(solution)/shard_map/all_to_all | solution.py:389
  78.3 0.3 sums.1
  78.6 14.7 %all_to_all.23 = f32[128,1,128]{2,1,0:T(1,128)S(1)} all-to-all(f32[128,1,128]{2,1,0:T(1,128)S(1)} %bitcast.11), channel_id=1, replica_groups=mesh['coil'=8,'space'=16] {'space','coil'}, dimensions={0} | all-to-all | bytes 131072 | tf_op jit(solution)/shard_map/all_to_all | solution.py:405
  93.3 1.1 %final.1 = (f32[2,8,32,64]{3,2,1,0:T(8,128)}, f32[2,8,32,64]{3,2,1,0:T(8,128)}, f32[2,8,32,64]{3,2,1,0:T(8,128)}) custom-call(f32[128,128]{1,0:T(8,128)S(1)} %bitcast.10, f32[8,32,128]{2,1,0:T(8,128)S(1)} %get-tuple-element.16.applied_ref, f32[3,8,32,128]{3,2,1,0:T(8,128)S(1)} %get-tuple-element.14.own_ref), custom_call_target="tpu_custom_call" | custom-call | tf_op jit(solution)/shard_map/final/pallas_call | solution.py:406
  (2 shorter events, 0.0 us)
Async XLA Ops:
  3.5 46.7 %copy-start = (f32[2,8,32,512]{3,2,1,0:T(8,128)S(1)}, f32[2,8,32,512]{3,2,1,0:T(8,128)}, u32[]{:S(2)}) copy-start(f32[2,8,32,512]{3,2,1,0:T(8,128)} %dir_ref.3) | copy-start | bytes 3145732
  3.5 46.7 %copy-start.1 = (bf16[512,512]{1,0:T(8,128)(2,1)S(1)}, bf16[512,512]{1,0:T(8,128)(2,1)}, u32[]{:S(2)}) copy-start(bf16[512,512]{1,0:T(8,128)(2,1)} %constant.41.clone.pick_ref) | copy-start | bytes 1572868
  3.5 46.7 %copy-start.2 = (bf16[2,512,256]{2,1,0:T(8,128)(2,1)S(1)}, bf16[2,512,256]{2,1,0:T(8,128)(2,1)}, u32[]{:S(2)}) copy-start(bf16[2,512,256]{2,1,0:T(8,128)(2,1)} %constant.40.clone.fold_t_ref) | copy-start | bytes 1572868
  3.5 46.7 %copy-start.3 = (bf16[512,512]{1,0:T(8,128)(2,1)S(1)}, bf16[512,512]{1,0:T(8,128)(2,1)}, u32[]{:S(2)}) copy-start(bf16[512,512]{1,0:T(8,128)(2,1)} %constant.39.clone.fold_ref) | copy-start | bytes 1572868
  3.5 46.7 %copy-start.4 = (f32[2,8,32,512]{3,2,1,0:T(8,128)S(1)}, f32[2,8,32,512]{3,2,1,0:T(8,128)}, u32[]{:S(2)}) copy-start(f32[2,8,32,512]{3,2,1,0:T(8,128)} %res_ref.1) | copy-start | bytes 3145732
  3.5 46.7 %copy-start.5 = (f32[2,8,32,512]{3,2,1,0:T(8,128)S(1)}, f32[2,8,32,512]{3,2,1,0:T(8,128)}, u32[]{:S(2)}) copy-start(f32[2,8,32,512]{3,2,1,0:T(8,128)} %img_ref.1) | copy-start | bytes 3145732
  48.3 3.9 %copy-start.6 = (bf16[512,512]{1,0:T(8,128)(2,1)S(1)}, bf16[512,512]{1,0:T(8,128)(2,1)}, u32[]{:S(2)}) copy-start(bf16[512,512]{1,0:T(8,128)(2,1)} %constant.45.clone.y_odd_ref) | copy-start | bytes 1572868
  48.3 3.9 %copy-start.7 = (bf16[512,512]{1,0:T(8,128)(2,1)S(1)}, bf16[512,512]{1,0:T(8,128)(2,1)}, u32[]{:S(2)}) copy-start(bf16[512,512]{1,0:T(8,128)(2,1)} %constant.44.clone.y_even_ref) | copy-start | bytes 1572868
  48.3 3.9 %copy-start.8 = (bf16[4,256,256]{2,1,0:T(8,128)(2,1)S(1)}, bf16[4,256,256]{2,1,0:T(8,128)(2,1)}, u32[]{:S(2)}) copy-start(bf16[4,256,256]{2,1,0:T(8,128)(2,1)} %constant.43.clone.z_back_ref) | copy-start | bytes 1572868
  48.3 3.9 %copy-start.9 = (bf16[512,512]{1,0:T(8,128)(2,1)S(1)}, bf16[512,512]{1,0:T(8,128)(2,1)}, u32[]{:S(2)}) copy-start(bf16[512,512]{1,0:T(8,128)(2,1)} %constant.42.clone.pick_t_ref) | copy-start | bytes 1572868
  48.3 3.9 %collective-permute-start = (bf16[16,48,512]{2,1,0:T(8,128)(2,1)S(1)}, bf16[16,48,512]{2,1,0:T(8,128)(2,1)S(1)}, u32[]{:S(2)}, u32[]{:S(2)}) collective-permute-start(bf16[16,48,512]{2,1,0:T(8,128)(2,1)S(1)} %slice.4), channel_id=1, source_target_pairs={{0,16},{16,0},{32,48},{48,32},{64,80},{80,64},{96,112},{112,96},{1... | collective-permute-start | bytes 2359304 | tf_op jit(solution)/shard_map/ppermute | solution.py:385
  57.7 2.0 %collective-permute-start.1 = (bf16[16,4,32,128]{3,2,1,0:T(8,128)(2,1)S(1)}, bf16[16,4,32,128]{3,2,1,0:T(8,128)(2,1)S(1)}, u32[]{:S(2)}, u32[]{:S(2)}) collective-permute-start(bf16[16,4,32,128]{3,2,1,0:T(8,128)(2,1)S(1)} %get-tuple-element.13), channel_id=1, source_target_pairs={{0,16},{16,0},{32,48},{48,32},{64,80},{80,64},{96,112},{112,96},{1... | collective-permute-start | bytes 1572872 | tf_op jit(solution)/shard_map/ppermute | solution.py:388

commit v8 on v7

--- a/solution.py
+++ b/solution.py
@@ -169,9 +169,9 @@
     def store(coil, part, start, value):
         spec_s[coil, part, :, pl.ds(start, 128)] = value
 
+    mask_ref[...] = mask_columns(got_ref[:, pl.ds(160, 16), :], pick_ref)
     dir_parts = [got_ref.at[:, pl.ds(128 + part * 16, 16), :] for part in range(2)]
     spectrum_rows(got_ref, dir_parts, core, fold_ref, image_s, store)
-    mask_ref[...] = mask_columns(got_ref[:, pl.ds(160, 16), :], pick_ref)
     for coil in range(2):
         for part in range(2):
             share_ref[coil, part] = dot(fold_t_ref[core], spec_s[coil, part])

time: 94.7 us -> 94.7 us (level)
  no operation moved by 1% of the time
where the time goes in v8:
time: 94.7 us; the launch traced here: 94.4 us
  blocking collectives  77.9 us (82%)
  Pallas kernels  11.6 us (12%)
  starting transfers between devices  2.24 us (2%)
  waiting for transfers between devices  1.63 us (2%)
    all_to_all x1, blocking collectives, on_device(): lax.all_to_all(packed.reshape(16, 176, 512), 'space', 0, 0, tiled=True)  44.7 us
    all_to_all x1, blocking collectives, on_device(): lax.all_to_all(pair_sum.reshape(64, 32, 128), ('coil', 'space'), 0, 0, ax...  18.5 us
    all_to_all x1, blocking collectives, on_device(): lax.all_to_all(sums, ('space', 'coil'), split_axis=0, concat_axis=0, tile...  14.7 us
    pallas_call x1, Pallas kernels, operator(): pl.pallas_call(operator_kernel, in_specs=[smem] + [vmem] * 11, out_specs=...  5.43 us
    pallas_call x1, Pallas kernels, pack(): pl.pallas_call(pack_kernel, in_specs=[pl.BlockSpec(memory_space=pltpu.SME...  2.82 us
    pallas_call x1, Pallas kernels, own_rows(): pl.pallas_call(own_rows_kernel, in_specs=[pl.BlockSpec(memory_space=pltpu...  1.93 us
  transfers between devices with their start and end apart: 2, of which 1 were waited for; matrix products, arithmetic and copies ran while one was open for 0% of the time, Pallas kernels for 2%

profile of v8, /device:TPU:1, one launch (start us, length us, event | category | flops | bytes accessed | tf_op | source)
XLA Modules:
  0.0 94.4 jit_solution(8418612299487670288)
XLA Ops:
  0.6 2.8 %pack.1 = bf16[8,2,176,512]{3,2,1,0:T(8,128)(2,1)} custom-call(s32[1]{0:T(128)S(6)} %select_n.7.core_ref, bf16[2,4,8,32,512]{4,3,2,1,0:T(8,128)(2,1)} %sens_ref.1, f32[2,8,32,512]{3,2,1,0:T(8,128)} %dir_ref.3, s32[32,512]{1,0:T(8,128)} %bitcast.14), custom_call_target="tpu_custom_call" | custom-call | tf_op jit(solution)/shard_map/pack/pallas_call | solution.py:102
  3.5 0.0 copy-start
  3.5 0.0 copy-start.1
  3.5 0.0 copy-start.2
  3.5 0.0 copy-start.3
  3.5 0.0 copy-start.4
  3.5 0.0 copy-start.5
  3.5 44.7 %all_to_all.21.got_ref = bf16[16,176,512]{2,1,0:T(8,128)(2,1)S(1)} all-to-all(bf16[16,176,512]{2,1,0:T(8,128)(2,1)} %bitcast.12), channel_id=1, replica_groups=mesh['coil'=8,'space'=16] {'space'}, dimensions={0} | all-to-all | bytes 5767168 | tf_op jit(solution)/shard_map/all_to_all | solution.py:384
  48.2 0.1 slice.4
  48.3 0.0 copy-start.6
  48.3 0.0 copy-start.7
  48.3 0.0 copy-start.8
  48.3 0.0 copy-start.9
  48.3 1.9 %collective-permute-start = (bf16[16,48,512]{2,1,0:T(8,128)(2,1)S(1)}, bf16[16,48,512]{2,1,0:T(8,128)(2,1)S(1)}, u32[]{:S(2)}, u32[]{:S(2)}) collective-permute-start(bf16[16,48,512]{2,1,0:T(8,128)(2,1)S(1)} %slice.4), channel_id=1, source_target_pairs={{0,16},{16,0},{32,48},{48,32},{64,80},{80,64},{96,112},{112,96},{1... | collective-permute-start | bytes 2359304 | tf_op jit(solution)/shard_map/ppermute | solution.py:385
  50.2 0.0 copy-done
  50.2 0.0 copy-done.1
  50.2 0.0 copy-done.2
  50.2 0.0 copy-done.3
  50.2 0.0 copy-done.4
  50.2 0.0 copy-done.5
  50.2 1.9 %own_rows.1 = (f32[2,2,512,512]{3,2,1,0:T(8,128)S(1)}, bf16[16,16,512]{2,1,0:T(8,128)(2,1)S(1)}, f32[3,8,32,128]{3,2,1,0:T(8,128)S(1)}) custom-call(s32[1]{0:T(128)} %bitcast.coil_ref, bf16[16,176,512]{2,1,0:T(8,128)(2,1)S(1)} %all_to_all.21.got_ref, bf16[512,512]{1,0:T(8,128)(2,1)S(1)} %copy-done.3, bf16[2,512,256]{2,1,0:T(8,128)(2,1)S(1)} %copy-done.2, ...), custom_call_target="tpu_custom_call" | custom-call | tf_op jit(solution)/shard_map/own_rows/pallas_call | solution.py:198
  52.2 0.0 collective-permute-done.mate_ref
  52.2 0.0 copy-done.6
  52.2 0.0 copy-done.7
  52.2 5.4 %operator.1 = (f32[16,4,32,128]{3,2,1,0:T(8,128)S(1)}, bf16[16,4,32,128]{3,2,1,0:T(8,128)(2,1)S(1)}) custom-call(s32[1]{0:T(128)} %bitcast.coil_ref, bf16[16,176,512]{2,1,0:T(8,128)(2,1)S(1)} %all_to_all.21.got_ref, bf16[16,48,512]{2,1,0:T(8,128)(2,1)S(1)} %collective-permute-done.mate_ref, f32[2,2,512,512]{3,2,1,0:T(8,128)S(1)} %get-tuple-element.10.share_ref, ...), custom_call_target="tpu_custom_call" | custom-call | tf_op jit(solution)/shard_map/operator/pallas_call | solution.py:313
  57.7 0.4 collective-permute-start.1
  58.0 1.6 %collective-permute-done.1 = bf16[16,4,32,128]{3,2,1,0:T(8,128)(2,1)S(1)} collective-permute-done((bf16[16,4,32,128]{3,2,1,0:T(8,128)(2,1)S(1)}, bf16[16,4,32,128]{3,2,1,0:T(8,128)(2,1)S(1)}, u32[]{:S(2)}, u32[]{:S(2)}) %collective-permute-start.1) | collective-permute-done | bytes 524320 | tf_op jit(solution)/shard_map/ppermute | solution.py:388
  59.7 0.2 add_convert_fusion
  59.8 18.5 %all_to_all.22 = bf16[64,32,128]{2,1,0:T(8,128)(2,1)S(1)} all-to-all(bf16[64,32,128]{2,1,0:T(8,128)(2,1)S(1)} %bitcast.13), channel_id=1, replica_groups={{0,32,64,96,1,33,65,97,2,34,66,98,3,35,67,99,4,36,68,100,5,37,69,101,6,..., dimensions={0} | all-to-all | bytes 1048576 | tf_op jit(solution)/shard_map/all_to_all | solution.py:389
  78.3 0.3 sums.1
  78.6 14.7 %all_to_all.23 = f32[128,1,128]{2,1,0:T(1,128)S(1)} all-to-all(f32[128,1,128]{2,1,0:T(1,128)S(1)} %bitcast.11), channel_id=1, replica_groups=mesh['coil'=8,'space'=16] {'space','coil'}, dimensions={0} | all-to-all | bytes 131072 | tf_op jit(solution)/shard_map/all_to_all | solution.py:405
  93.3 1.1 %final.1 = (f32[2,8,32,64]{3,2,1,0:T(8,128)}, f32[2,8,32,64]{3,2,1,0:T(8,128)}, f32[2,8,32,64]{3,2,1,0:T(8,128)}) custom-call(f32[128,128]{1,0:T(8,128)S(1)} %bitcast.10, f32[8,32,128]{2,1,0:T(8,128)S(1)} %get-tuple-element.16.applied_ref, f32[3,8,32,128]{3,2,1,0:T(8,128)S(1)} %get-tuple-element.14.own_ref), custom_call_target="tpu_custom_call" | custom-call | tf_op jit(solution)/shard_map/final/pallas_call | solution.py:406
  (2 shorter events, 0.0 us)
Async XLA Ops:
  3.5 46.7 %copy-start = (f32[2,8,32,512]{3,2,1,0:T(8,128)S(1)}, f32[2,8,32,512]{3,2,1,0:T(8,128)}, u32[]{:S(2)}) copy-start(f32[2,8,32,512]{3,2,1,0:T(8,128)} %dir_ref.3) | copy-start | bytes 3145732
  3.5 46.7 %copy-start.1 = (bf16[512,512]{1,0:T(8,128)(2,1)S(1)}, bf16[512,512]{1,0:T(8,128)(2,1)}, u32[]{:S(2)}) copy-start(bf16[512,512]{1,0:T(8,128)(2,1)} %constant.41.clone.pick_ref) | copy-start | bytes 1572868
  3.5 46.7 %copy-start.2 = (bf16[2,512,256]{2,1,0:T(8,128)(2,1)S(1)}, bf16[2,512,256]{2,1,0:T(8,128)(2,1)}, u32[]{:S(2)}) copy-start(bf16[2,512,256]{2,1,0:T(8,128)(2,1)} %constant.40.clone.fold_t_ref) | copy-start | bytes 1572868
  3.5 46.7 %copy-start.3 = (bf16[512,512]{1,0:T(8,128)(2,1)S(1)}, bf16[512,512]{1,0:T(8,128)(2,1)}, u32[]{:S(2)}) copy-start(bf16[512,512]{1,0:T(8,128)(2,1)} %constant.39.clone.fold_ref) | copy-start | bytes 1572868
  3.5 46.7 %copy-start.4 = (f32[2,8,32,512]{3,2,1,0:T(8,128)S(1)}, f32[2,8,32,512]{3,2,1,0:T(8,128)}, u32[]{:S(2)}) copy-start(f32[2,8,32,512]{3,2,1,0:T(8,128)} %res_ref.1) | copy-start | bytes 3145732
  3.5 46.7 %copy-start.5 = (f32[2,8,32,512]{3,2,1,0:T(8,128)S(1)}, f32[2,8,32,512]{3,2,1,0:T(8,128)}, u32[]{:S(2)}) copy-start(f32[2,8,32,512]{3,2,1,0:T(8,128)} %img_ref.1) | copy-start | bytes 3145732
  48.3 3.9 %copy-start.6 = (bf16[512,512]{1,0:T(8,128)(2,1)S(1)}, bf16[512,512]{1,0:T(8,128)(2,1)}, u32[]{:S(2)}) copy-start(bf16[512,512]{1,0:T(8,128)(2,1)} %constant.45.clone.y_odd_ref) | copy-start | bytes 1572868
  48.3 3.9 %copy-start.7 = (bf16[512,512]{1,0:T(8,128)(2,1)S(1)}, bf16[512,512]{1,0:T(8,128)(2,1)}, u32[]{:S(2)}) copy-start(bf16[512,512]{1,0:T(8,128)(2,1)} %constant.44.clone.y_even_ref) | copy-start | bytes 1572868
  48.3 3.9 %copy-start.8 = (bf16[4,256,256]{2,1,0:T(8,128)(2,1)S(1)}, bf16[4,256,256]{2,1,0:T(8,128)(2,1)}, u32[]{:S(2)}) copy-start(bf16[4,256,256]{2,1,0:T(8,128)(2,1)} %constant.43.clone.z_back_ref) | copy-start | bytes 1572868
  48.3 3.9 %copy-start.9 = (bf16[512,512]{1,0:T(8,128)(2,1)S(1)}, bf16[512,512]{1,0:T(8,128)(2,1)}, u32[]{:S(2)}) copy-start(bf16[512,512]{1,0:T(8,128)(2,1)} %constant.42.clone.pick_t_ref) | copy-start | bytes 1572868
  48.3 3.9 %collective-permute-start = (bf16[16,48,512]{2,1,0:T(8,128)(2,1)S(1)}, bf16[16,48,512]{2,1,0:T(8,128)(2,1)S(1)}, u32[]{:S(2)}, u32[]{:S(2)}) collective-permute-start(bf16[16,48,512]{2,1,0:T(8,128)(2,1)S(1)} %slice.4), channel_id=1, source_target_pairs={{0,16},{16,0},{32,48},{48,32},{64,80},{80,64},{96,112},{112,96},{1... | collective-permute-start | bytes 2359304 | tf_op jit(solution)/shard_map/ppermute | solution.py:385
  57.7 2.0 %collective-permute-start.1 = (bf16[16,4,32,128]{3,2,1,0:T(8,128)(2,1)S(1)}, bf16[16,4,32,128]{3,2,1,0:T(8,128)(2,1)S(1)}, u32[]{:S(2)}, u32[]{:S(2)}) collective-permute-start(bf16[16,4,32,128]{3,2,1,0:T(8,128)(2,1)S(1)} %get-tuple-element.13), channel_id=1, source_target_pairs={{0,16},{16,0},{32,48},{48,32},{64,80},{80,64},{96,112},{112,96},{1... | collective-permute-start | bytes 1572872 | tf_op jit(solution)/shard_map/ppermute | solution.py:388
